TPU v7x, 512 devices: a whole 4x4x16 slice. The times are simulated.
512 devices in a mesh: prompt: 8 (over z_lo, core), resp: 16 (over z_hi, x), tensor: 4 (over y).
Axes of the slice: x: 4, y: 4, z: 16 (z_hi: 4, z_lo: 4; z = z_hi * 4 + z_lo), core: 2. Of those that a mesh axis runs over, the one named last changes fastest.
Arguments:
- queries: bfloat16 [128, 2, 64, 96, 128], P(('prompt', 'resp'), None, None, 'tensor'), may hold values from -192 to 192
- resp_kv: bfloat16 [128, 2, 64, 8, 2, 128], P(('prompt', 'resp'), None, None, 'tensor'), may hold values from -6 to 6
- prompt_kv: bfloat16 [16, 1024, 8, 2, 128], P('resp', 'prompt', 'tensor'), may hold values from -6 to 6
- prompt_of: int32 [128], replicated, may hold values from 0 to 15
- prompt_len: int32 [16], replicated, may hold values from 1 to 8, as said below
- reward_head: float32 [96, 128], P('tensor'), may hold values from -0.0546875 to 0.0546875
Outputs:
- pair_loss: float32 [128], P(('prompt', 'resp'))
- grad_query: bfloat16 [128, 2, 64, 96, 128], P(('prompt', 'resp'), None, None, 'tensor')
- grad_resp_kv: bfloat16 [128, 2, 64, 8, 2, 128], P(('prompt', 'resp'), None, None, 'tensor')
- grad_prompt_kv: bfloat16 [16, 1024, 8, 2, 128], P('resp', 'prompt', 'tensor')
Inputs may be any that keep to these rules, and one draw needn't show every extreme that they name: `prompt_len`: at least one prompt has all 8 blocks.
All inputs are finite; a program needn't handle non-finite values.
Results may differ from a plain program's by a relative error of at most 0.025.
Values may be sent and summed in bfloat16 or wider, within the bound.
A program may use at most 128 MiB of HBM per device.

v0:
```python
import jax
import jax.numpy as jnp
from jax import lax
from jax.sharding import PartitionSpec as P

BLOCK = 128


loss_scale = 8192.0


def product(form, left, right):
    return jnp.einsum(form, left, right, preferred_element_type=jnp.float32)


def block_probs(head_rows, key_rows, allowed):
    scores = product("igd,cd->gic", head_rows, key_rows) * head_rows.shape[-1] ** (-0.5)
    scores = jnp.where(allowed[None], scores, -1e30)
    highest = jnp.max(scores, axis=-1, keepdims=True)
    exponent = jnp.exp(scores - highest)
    return exponent / jnp.sum(exponent, axis=-1, keepdims=True)


def add_heads(partial_value):
    return lax.psum(partial_value, "tensor")


def pair_pass(pair_queries, pair_kv, prompt_rows, length, head_weight):
    positions = pair_queries.shape[1]
    prompt_span = prompt_rows.shape[0]
    kv_local = pair_kv.shape[2]
    group_size = pair_queries.shape[2] // kv_local
    score_scale = pair_queries.shape[-1] ** (-0.5)
    prompt_seen = jnp.arange(prompt_span) < length * BLOCK
    causal = jnp.arange(positions)[None, :] <= jnp.arange(positions)[:, None]
    allowed = jnp.concatenate(
        [jnp.broadcast_to(prompt_seen[None, :], (positions, prompt_span)), causal], axis=1
    )
    blocks = []
    for member in range(2):
        for kv_head in range(kv_local):
            key_rows = jnp.concatenate(
                [prompt_rows[:, kv_head, 0], pair_kv[member, :, kv_head, 0]], axis=0
            )
            value_rows = jnp.concatenate(
                [prompt_rows[:, kv_head, 1], pair_kv[member, :, kv_head, 1]], axis=0
            )
            head_rows = pair_queries[member, :, kv_head * group_size : (kv_head + 1) * group_size]
            blocks.append((member, kv_head, head_rows, key_rows, value_rows))
    outputs = {}
    kept = {}
    for member, kv_head, head_rows, key_rows, value_rows in blocks:
        weights = block_probs(head_rows, key_rows, allowed)
        rounded = weights.astype(jnp.bfloat16)
        kept[member, kv_head] = (weights, rounded)
        outputs[member, kv_head] = product("gic,cd->igd", rounded, value_rows).astype(jnp.bfloat16)
    partial_value = (
        jnp.stack(
            [
                jnp.sum(
                    jnp.concatenate(
                        [outputs[member, kv_head] for kv_head in range(kv_local)], axis=1
                    ).astype(jnp.float32)
                    * head_weight[None]
                )
                for member in range(2)
            ]
        )
        / positions
    )
    reward = add_heads(partial_value)
    margin = reward[1] - reward[0]
    pair_loss = jnp.logaddexp(0.0, margin)
    sigmoid_gap = jax.nn.sigmoid(margin)
    slopes = (-sigmoid_gap, sigmoid_gap)
    grad_query = [[None] * kv_local for member in range(2)]
    grad_resp = [[None] * kv_local for member in range(2)]
    grad_prompt = [None] * kv_local
    for member, kv_head, head_rows, key_rows, value_rows in blocks:
        weights, rounded = kept[member, kv_head]
        head_part = head_weight[kv_head * group_size : (kv_head + 1) * group_size]
        d_head = (loss_scale * slopes[member] / positions * head_part).astype(jnp.bfloat16)
        out_block = outputs[member, kv_head]
        d_probs = product("gd,cd->gc", d_head, value_rows)
        row_delta = jnp.einsum(
            "gd,igd->gi",
            d_head.astype(jnp.float32),
            out_block.astype(jnp.float32),
            precision=lax.Precision.HIGHEST,
        )
        d_scores = (weights * (d_probs[:, None, :] - row_delta[:, :, None])).astype(jnp.bfloat16)
        grad_query[member][kv_head] = (
            product("gic,cd->igd", d_scores, key_rows) * score_scale
        ).astype(jnp.bfloat16)
        grad_k = product("gic,igd->cd", d_scores, head_rows) * score_scale
        column_sums = jnp.sum(rounded.astype(jnp.float32), axis=1)
        grad_v = jnp.einsum(
            "gc,gd->cd", column_sums, d_head.astype(jnp.float32), precision=lax.Precision.HIGHEST
        )
        grad_resp[member][kv_head] = jnp.stack(
            [grad_k[prompt_span:], grad_v[prompt_span:]], axis=1
        ).astype(jnp.bfloat16)
        prompt_term = jnp.stack([grad_k[:prompt_span], grad_v[:prompt_span]], axis=1)
        grad_prompt[kv_head] = (
            prompt_term if grad_prompt[kv_head] is None else grad_prompt[kv_head] + prompt_term
        )
    query_out = jnp.stack(
        [jnp.concatenate(grad_query[member], axis=1) for member in range(2)], axis=0
    )
    resp_out = jnp.stack([jnp.stack(grad_resp[member], axis=1) for member in range(2)], axis=0)
    prompt_out = jnp.stack(grad_prompt, axis=1)
    return (pair_loss, query_out, resp_out, prompt_out)


def shards(queries, resp_kv, prompt_kv, prompt_of, prompt_len, reward_head):
    n_resp = lax.axis_size("resp")
    n_prompt = lax.axis_size("prompt")
    pair_index = lax.axis_index(("prompt", "resp"))
    resp_index = lax.axis_index("resp")
    prompt_id = prompt_of[pair_index]
    table = prompt_of.reshape(n_prompt, n_resp)
    column = lax.dynamic_index_in_dim(table, resp_index, 1, keepdims=False)
    every_prompt = lax.all_gather(prompt_kv, "resp", axis=0, tiled=True)
    picked = jnp.take(every_prompt, column, axis=0)
    arrived = lax.all_to_all(picked, "prompt", split_axis=0, concat_axis=0, tiled=True)
    whole = arrived.reshape((-1,) + arrived.shape[2:])
    length = prompt_len[prompt_id]
    pair_loss, query_out, resp_out, prompt_out = pair_pass(
        queries[0], resp_kv[0], whole, length, reward_head
    )
    pieces = prompt_out.reshape((n_prompt, -1) + prompt_out.shape[1:])
    returned = lax.all_to_all(
        pieces.astype(jnp.bfloat16), "prompt", split_axis=0, concat_axis=0, tiled=True
    ).astype(pieces.dtype)
    selector = (column[:, None] == jnp.arange(n_resp)[None, :]).astype(jnp.float32)
    dense = jnp.einsum("pn,prkjd->nrkjd", selector, returned, precision=lax.Precision.HIGHEST)
    owned = lax.psum_scatter(dense.astype(jnp.bfloat16), "resp", scatter_dimension=0, tiled=True)
    return (pair_loss[None], query_out[None], resp_out[None], owned)


def solution(mesh):
    in_specs = (
        P(("prompt", "resp"), None, None, "tensor", None),
        P(("prompt", "resp"), None, None, "tensor", None, None),
        P("resp", "prompt", "tensor", None, None),
        P(),
        P(),
        P("tensor", None),
    )
    out_specs = (
        P(("prompt", "resp")),
        P(("prompt", "resp"), None, None, "tensor", None),
        P(("prompt", "resp"), None, None, "tensor", None, None),
        P("resp", "prompt", "tensor", None, None),
    )
    return jax.shard_map(shards, mesh=mesh, in_specs=in_specs, out_specs=out_specs, check_vma=False)
```

profile of v0, /device:TPU:1, one launch (start us, length us, event | category | flops | bytes accessed | tf_op | source)
XLA Modules:
  0.0 380.4 jit_solution(654158439786896048)
XLA Ops:
  7.2 1.7 copy.38
  8.9 0.7 reshape.312
  9.7 0.7 dynamic-slice_reduce_fusion
  10.6 100.5 %all-gather.2.cloned.1.call-done = bf16[16,128,2,2,128]{4,1,3,2,0:T(8,128)(2,1)} async-done(((bf16[1,128,2,2,128]{4,1,3,2,0:T(8,128)(2,1)}), bf16[16,128,2,2,128]{4,1,3,2,0:T(8,128)(2,1)}) %all-gather.2.cloned.1.call-update) | async-done | bytes 2097168 | tf_op jit(solution)/shard_map/all_gather | solution.py:123
  111.1 2.3 gather_fusion
  113.5 1.1 broadcast_select_fusion
  114.6 4.9 %all-to-all-start = ((bf16[8,128,2,2,128]{4,1,3,2,0:T(8,128)(2,1)}), bf16[8,128,2,2,128]{4,1,3,2,0:T(8,128)(2,1)S(1)}, u32[]{:S(2)}, u32[]{:S(2)}) async-start(bf16[8,128,2,2,128]{4,1,3,2,0:T(8,128)(2,1)} %broadcast_select_fusion), calls=%async_computation | async-start | bytes 2097152 | tf_op jit(solution)/shard_map/all_to_all | solution.py:125
  123.6 0.7 slice_bitcast_fusion.35
  124.3 21.0 %all-to-all-done = bf16[8,128,2,2,128]{4,1,3,2,0:T(8,128)(2,1)S(1)} async-done(((bf16[8,128,2,2,128]{4,1,3,2,0:T(8,128)(2,1)}), bf16[8,128,2,2,128]{4,1,3,2,0:T(8,128)(2,1)S(1)}, u32[]{:S(2)}, u32[]{:S(2)}) %all-to-all-start) | async-done | bytes 1048608 | tf_op jit(solution)/shard_map/all_to_all | solution.py:125
  145.4 0.9 slice_bitcast_fusion.3
  146.3 3.9 %fusion.108 = (f32[12,64]{1,0:T(8,128)}, f32[12,64,1088]{2,1,0:T(8,128)}) fusion(pred[64,1088]{1,0:T(8,128)(4,1)S(1)} %pad_add_fusion, bf16[2,64,24,128]{3,1,2,0:T(8,128)(2,1)S(1)} %bitcast.299, bf16[64,128]{1,0:T(8,128)(2,1)S(1)} %get-tuple-element.36, bf16[1024,128]{1,0:T(8,128)(2,1)S(1)} %get-tuple-element.29), kind=kOutput, calls=%fused_computation.192 | convolution fusion | flops 217809984 | bytes 3894272 | tf_op jit(solution)/shard_map/sub | solution.py:20
  150.2 3.8 fusion.110
  153.9 3.1 fusion.109
  157.1 4.2 %fusion.111 = (f32[12,64]{1,0:T(8,128)S(1)}, f32[12,64,1088]{2,1,0:T(8,128)}) fusion(pred[64,1088]{1,0:T(8,128)(4,1)} %copy-done.38, bf16[2,64,24,128]{3,1,2,0:T(8,128)(2,1)} %bitcast.302, bf16[64,128]{1,0:T(8,128)(2,1)} %get-tuple-element.35, bf16[1024,128]{1,0:T(8,128)(2,1)} %get-tuple-element.31), kind=kOutput, calls=%fused_computation.195 | convolution fusion | flops 217809984 | bytes 3894272 | tf_op jit(solution)/shard_map/sub | solution.py:20
  161.3 3.3 convert_reduce_fusion.2
  164.6 1.3 convert_reduce_fusion.3
  165.9 0.7 copy-done
  166.6 1.3 convert_reduce_fusion
  169.3 0.7 copy-done.2
  170.0 1.3 convert_reduce_fusion.1
  172.0 0.6 convolution_convert_fusion.2
  172.7 0.9 multiply_reduce_fusion.1
  173.6 2.0 maximum_multiply_fusion
  175.6 8.0 %psum.7 = f32[2]{0:T(128)S(1)} all-reduce(f32[2]{0:T(128)} %maximum_multiply_fusion), channel_id=1, replica_groups=mesh['prompt'=8,'resp'=16,'tensor'=4] {'tensor'}, use_global_device_ids=true, to_apply=%region_10.11 | all-reduce | flops 2 | bytes 16 | tf_op jit(solution)/shard_map/psum | solution.py:25
  183.6 0.7 fusion.107
  185.7 1.1 fusion.46
  186.8 1.1 fusion.65
  188.0 1.2 fusion.43
  189.2 1.2 fusion.59
  190.4 1.2 fusion.44
  191.5 1.1 fusion.61
  192.7 1.2 fusion.45
  193.9 1.1 fusion.63
  195.0 2.6 multiply_convert_fusion.2
  197.7 0.6 fusion.22
  198.4 2.2 copy-done.1
  201.2 0.6 fusion.20
  201.8 2.2 copy-done.3
  204.0 0.6 multiply_convert_fusion.1
  204.6 0.6 fusion.21
  205.4 0.6 multiply_convert_fusion.3
  206.0 0.7 fusion.23
  207.0 0.6 fusion.113
  207.7 0.6 fusion.115
  208.4 0.6 fusion.114
  209.2 0.6 fusion.112
  209.8 0.8 copy-done.17
  210.8 3.7 fusion.36
  214.5 1.5 pad_maximum_fusion
  216.0 30.9 %all_to_all.10 = bf16[8,128,2,2,128]{4,3,2,1,0:T(2,128)(2,1)S(1)} all-to-all(bf16[8,128,2,2,128]{4,3,2,1,0:T(2,128)(2,1)S(1)} %pad_maximum_fusion), channel_id=1, replica_groups=mesh['prompt'=8,'resp'=16,'tensor'=4] {'prompt'}, dimensions={0} | all-to-all | bytes 2097152 | tf_op jit(solution)/shard_map/all_to_all | solution.py:132
  246.8 1.0 convolution_convert_fusion
  247.9 2.7 copy.51
  250.8 1.7 fusion.34
  252.5 1.6 fusion.32
  254.1 0.6 fusion.33
  254.8 0.6 fusion.35
  255.6 1.4 copy.52
  257.0 0.8 fusion.57
  257.8 0.8 fusion.55
  258.6 0.8 fusion.53
  259.3 0.8 fusion.51
  260.2 0.8 copy.53
  260.9 109.8 %reduce-scatter.2.cloned.1.call-done = bf16[1,128,2,2,128]{4,1,3,2,0:T(8,128)(2,1)} async-done(((bf16[16,128,2,2,128]{4,1,3,2,0:T(8,128)(2,1)}), bf16[1,128,2,2,128]{4,1,3,2,0:T(8,128)(2,1)}) %reduce-scatter.2.cloned.1.call-update) | async-done | bytes 131088 | tf_op jit(solution)/shard_map/reduce_scatter | solution.py:137
  370.8 1.7 copy.54
  (152 shorter events, 5.2 us)
Async XLA Ops:
  7.2 112.4 %copy-start.57 = (s32[128]{0:T(128)S(1)}, s32[128]{0:T(128)}, u32[]{:S(2)}) copy-start(s32[128]{0:T(128)} %param.9) | copy-start | bytes 1540
  7.2 114.2 %copy-start.37 = (bf16[1,2,64,2,2,128]{5,4,3,2,1,0:T(2,128)(2,1)S(1)}, bf16[1,2,64,2,2,128]{5,4,3,2,1,0:T(2,128)(2,1)}, u32[]{:S(2)}) copy-start(bf16[1,2,64,2,2,128]{5,4,3,2,1,0:T(2,128)(2,1)} %param.7) | copy-start | bytes 393220
  7.2 114.3 %copy-start.24 = (bf16[1,2,64,24,128]{4,3,2,1,0:T(8,128)(2,1)S(1)}, bf16[1,2,64,24,128]{4,3,2,1,0:T(8,128)(2,1)}, u32[]{:S(2)}) copy-start(bf16[1,2,64,24,128]{4,3,2,1,0:T(8,128)(2,1)} %param.6) | copy-start | bytes 2359300
  7.2 103.9 %all-gather.2.cloned.1.call-start = ((), (), s32[]{:S(2)}) async-start(), calls=%async_computation.3 | async-start | bytes 2228224 | tf_op jit(solution)/shard_map/all_gather | solution.py:123
  113.5 8.8 %copy-start.58 = (s32[16]{0:T(128)S(1)}, s32[16]{0:T(128)}, u32[]{:S(2)}) copy-start(s32[16]{0:T(128)} %param.10) | copy-start | bytes 196
  114.6 30.6 %all-to-all-start = ((bf16[8,128,2,2,128]{4,1,3,2,0:T(8,128)(2,1)}), bf16[8,128,2,2,128]{4,1,3,2,0:T(8,128)(2,1)S(1)}, u32[]{:S(2)}, u32[]{:S(2)}) async-start(bf16[8,128,2,2,128]{4,1,3,2,0:T(8,128)(2,1)} %broadcast_select_fusion), calls=%async_computation | async-start | bytes 2097152 | tf_op jit(solution)/shard_map/all_to_all | solution.py:125
  119.5 251.3 %reduce-scatter.2.cloned.1.call-start = ((), (), s32[]{:S(2)}) async-start(), calls=%async_computation.4 | async-start | bytes 2228224 | tf_op jit(solution)/shard_map/reduce_scatter | solution.py:137
  121.6 28.5 %copy-start.25 = (bf16[1,2,64,24,128]{4,2,3,1,0:T(8,128)(2,1)}, bf16[1,2,64,24,128]{4,2,3,1,0:T(8,128)(2,1)S(1)}, u32[]{:S(2)}) copy-start(bf16[1,2,64,24,128]{4,2,3,1,0:T(8,128)(2,1)S(1)} %copy.80) | copy-start | bytes 2359300
  124.2 25.9 %copy-start.44 = (bf16[64,128]{1,0:T(8,128)(2,1)}, bf16[64,128]{1,0:T(8,128)(2,1)S(1)}, u32[]{:S(2)}) copy-start(bf16[64,128]{1,0:T(8,128)(2,1)S(1)} %get-tuple-element.36) | copy-start | bytes 49156
  124.3 25.9 %copy-start.43 = (bf16[64,128]{1,0:T(8,128)(2,1)}, bf16[64,128]{1,0:T(8,128)(2,1)S(1)}, u32[]{:S(2)}) copy-start(bf16[64,128]{1,0:T(8,128)(2,1)S(1)} %get-tuple-element.33) | copy-start | bytes 49156
  124.3 29.7 %copy-start.40 = (bf16[64,128]{1,0:T(8,128)(2,1)}, bf16[64,128]{1,0:T(8,128)(2,1)S(1)}, u32[]{:S(2)}) copy-start(bf16[64,128]{1,0:T(8,128)(2,1)S(1)} %get-tuple-element.38) | copy-start | bytes 49156
  124.3 25.9 %copy-start.38 = (pred[64,1088]{1,0:T(8,128)(4,1)}, pred[64,1088]{1,0:T(8,128)(4,1)S(1)}, u32[]{:S(2)}) copy-start(pred[64,1088]{1,0:T(8,128)(4,1)S(1)} %pad_add_fusion) | copy-start | bytes 208900
  146.3 7.7 %copy-start.13 = (bf16[1024,128]{1,0:T(8,128)(2,1)}, bf16[1024,128]{1,0:T(8,128)(2,1)S(1)}, u32[]{:S(2)}) copy-start(bf16[1024,128]{1,0:T(8,128)(2,1)S(1)} %get-tuple-element.29) | copy-start | bytes 786436
  157.1 4.2 %copy-start.55 = (f32[12,64]{1,0:T(8,128)S(1)}, f32[12,64]{1,0:T(8,128)}, u32[]{:S(2)}) copy-start(f32[12,64]{1,0:T(8,128)} %get-tuple-element.46) | copy-start | bytes 9220
  161.3 8.0 %copy-start.53 = (f32[12,64]{1,0:T(8,128)}, f32[12,64]{1,0:T(8,128)S(1)}, u32[]{:S(2)}) copy-start(f32[12,64]{1,0:T(8,128)S(1)} %get-tuple-element.52) | copy-start | bytes 9220
  161.3 3.3 copy-start.49
  164.6 2.0 copy-start
  164.6 2.0 copy-start.51
  165.9 2.1 copy-start.14
  165.9 2.1 copy-start.45
  166.6 2.0 copy-start.47
  168.0 2.1 copy-start.2
  168.6 4.1 %copy-start.27 = (bf16[128,12,64]{0,2,1:T(8,128)(2,1)}, bf16[128,12,64]{0,2,1:T(8,128)(2,1)S(1)}, u32[]{:S(2)}) copy-start(bf16[128,12,64]{0,2,1:T(8,128)(2,1)S(1)} %convolution_convert_fusion.3) | copy-start | bytes 589828
  168.6 2.7 copy-start.15
  168.6 2.7 copy-start.48
  169.3 3.4 copy-start.28
  170.0 2.0 copy-start.46
  171.4 1.3 copy-start.39
  172.0 1.6 copy-start.30
  172.7 1.0 copy-start.29
  189.2 8.5 %copy-start.26 = (bf16[1,2,64,24,128]{4,2,3,1,0:T(8,128)(2,1)S(1)}, bf16[1,2,64,24,128]{4,2,3,1,0:T(8,128)(2,1)}, u32[]{:S(2)}) copy-start(bf16[1,2,64,24,128]{4,2,3,1,0:T(8,128)(2,1)} %copy-done.25) | copy-start | bytes 2359300
  197.7 3.4 copy-start.4
  197.7 2.8 copy-start.1
  197.7 2.8 copy-start.52
  198.4 9.3 %copy-start.20 = (f32[1088,128]{1,0:T(8,128)}, f32[1088,128]{1,0:T(8,128)S(1)}, u32[]{:S(2)}) copy-start(f32[1088,128]{1,0:T(8,128)S(1)} %fusion.22) | copy-start | bytes 1671172
  201.1 3.5 copy-start.6
  201.1 2.8 copy-start.3
  201.1 2.8 copy-start.54
  201.8 6.6 %copy-start.22 = (f32[1088,128]{1,0:T(8,128)}, f32[1088,128]{1,0:T(8,128)S(1)}, u32[]{:S(2)}) copy-start(f32[1088,128]{1,0:T(8,128)S(1)} %fusion.20) | copy-start | bytes 1671172
  204.6 1.4 copy-start.8
  204.6 0.7 copy-start.50
  205.3 3.8 %copy-start.32 = (f32[1088,128]{1,0:T(8,128)}, f32[1088,128]{1,0:T(8,128)S(1)}, u32[]{:S(2)}) copy-start(f32[1088,128]{1,0:T(8,128)S(1)} %fusion.21) | copy-start | bytes 1671172
  206.0 1.7 copy-start.10
  206.0 1.0 copy-start.34
  206.0 1.7 copy-start.35
  206.7 4.0 %copy-start.31 = (f32[1088,128]{1,0:T(8,128)}, f32[1088,128]{1,0:T(8,128)S(1)}, u32[]{:S(2)}) copy-start(f32[1088,128]{1,0:T(8,128)S(1)} %fusion.23) | copy-start | bytes 1671172
  206.7 1.7 copy-start.36
  207.6 1.6 copy-start.16
  207.6 1.6 copy-start.33
  208.3 2.4 copy-start.18
  208.4 2.4 slice-start
  208.4 2.4 slice-start.1
  209.1 1.7 copy-start.19
  209.8 0.8 copy-start.17
  210.8 36.0 %copy-start.56 = (s32[8]{0:T(128)S(1)}, s32[8]{0:T(128)}, u32[]{:S(2)}) copy-start(s32[8]{0:T(128)} %get-tuple-element.18) | copy-start | bytes 100
  247.9 2.9 copy-start.5
  247.9 4.6 %copy-start.7 = (bf16[12,64,1088]{2,1,0:T(8,128)(2,1)S(1)}, bf16[12,64,1088]{2,1,0:T(8,128)(2,1)}, u32[]{:S(2)}) copy-start(bf16[12,64,1088]{2,1,0:T(8,128)(2,1)} %copy-done.6) | copy-start | bytes 5013508
  250.6 4.2 %copy-start.41 = (bf16[64,128]{1,0:T(8,128)(2,1)S(1)}, bf16[64,128]{1,0:T(8,128)(2,1)}, u32[]{:S(2)}) copy-start(bf16[64,128]{1,0:T(8,128)(2,1)} %copy-done.40) | copy-start | bytes 49156
  250.7 3.4 copy-start.9
  250.7 3.4 copy-start.12
  250.7 3.4 copy-start.42
  250.7 4.0 %copy-start.11 = (bf16[12,64,1088]{2,1,0:T(8,128)(2,1)S(1)}, bf16[12,64,1088]{2,1,0:T(8,128)(2,1)}, u32[]{:S(2)}) copy-start(bf16[12,64,1088]{2,1,0:T(8,128)(2,1)} %copy-done.10) | copy-start | bytes 5013508
  254.8 2.2 copy-start.23
  254.8 3.8 copy-start.21
Sparse Core Ops, SparseCore 0:
  11.6 99.4 all-gather.1
  250.7 119.9 reduce-scatter.1
where the time goes:
time: 381 us; the launch traced here: 380 us
  waiting for transfers between devices  231 us (61%)
  blocking collectives  38.9 us (10%)
  matrix products  37.5 us (10%)
  local copies, waits for them, and re-layouts  25.5 us (7%)
  other arithmetic  22 us (6%)
  between operations  20.2 us (5%)
  starting transfers between devices  4.93 us (1%)
    reduce_scatter x1, waiting for transfers between devices, shards(): lax.psum_scatter(dense.astype(jnp.bfloat16), 'resp', scatter_dimension=0,...  110 us
    all_gather x1, waiting for transfers between devices, shards(): every_prompt = lax.all_gather(prompt_kv, 'resp', axis=0, tiled=True)  101 us
    all_to_all x1, blocking collectives, shards(): lax.all_to_all(pieces.astype(jnp.bfloat16), 'prompt', split_axis=0, conca...  30.9 us
    all_to_all x1, waiting for transfers between devices, shards(): lax.all_to_all(picked, 'prompt', split_axis=0, concat_axis=0, tiled=True)  21 us
    sub x4, matrix products, block_probs(): exponent = jnp.exp(scores - highest)  15 us
    dot_general x16, matrix products, product(): return jnp.einsum(form, left, right, preferred_element_type=jnp.float32)  14.4 us
    unnamed x124, local copies, waits for them, and re-layouts  12.9 us
    psum x1, blocking collectives, add_heads(): return lax.psum(partial_value, 'tensor')  8.03 us
  transfers between devices with their start and end apart: 3, of which 3 were waited for; matrix products, arithmetic and copies ran while one was open for 4% of the time, Pallas kernels for 0%

commit v1 on v0

v1 whole, which is shorter than its diff:
```python
import math

import jax
import jax.numpy as jnp
from jax import lax
from jax.experimental import pallas as pl
from jax.experimental.pallas import tpu as pltpu
from jax.sharding import PartitionSpec as P

BLOCK = 128
TILE = 256

loss_scale = 8192.0


def product(left, right):
    return jnp.dot(left, right, preferred_element_type=jnp.float32)


def product_nt(left, right):
    return lax.dot_general(
        left, right, (((1,), (1,)), ((), ())), preferred_element_type=jnp.float32
    )


def attend_kernel(
    length_ref,
    q_ref,
    kv_ref,
    rkv_ref,
    w_ref,
    gq_ref,
    gp_ref,
    gr_ref,
    reward_ref,
    wrow_ref,
    wt_ref,
    mask_ref,
    mask_t_ref,
    w2_ref,
    kt_ref,
    vt_ref,
    rkt_ref,
    rvt_ref,
    dp_ref,
    drp_ref,
    s_ref,
    p_ref,
    ds_ref,
):
    members, rows, hd = q_ref.shape
    span = kv_ref.shape[0]
    positions = rkv_ref.shape[1]
    heads = w_ref.shape[0]
    blocks = span // BLOCK
    period = wrow_ref.shape[0]
    phases = period // TILE
    tiles = rows // TILE
    wide = 2 * hd
    scale = hd**-0.5
    pace = scale * math.log2(math.e)
    length = length_ref[0]

    for index in range(period // heads):
        wrow_ref[index * heads : (index + 1) * heads, :] = w_ref[...]
    for phase in range(phases):
        part = slice(phase * TILE, (phase + 1) * TILE)
        row = lax.broadcasted_iota(jnp.int32, (TILE, hd), 0) + phase * TILE
        first = (lax.rem(row, heads) < heads // 2).astype(jnp.float32)
        wrow = wrow_ref[part, :]
        mask_ref[part, :] = first.astype(jnp.bfloat16)
        mask_t_ref[:, part] = first.T
        wt_ref[:, part] = wrow.T
        w2 = jnp.concatenate([wrow * first, wrow * (1.0 - first)], axis=1)
        w2_ref[part, :] = w2.astype(jnp.bfloat16)
        w2t = w2.T.astype(jnp.bfloat16)
        dp_ref[:, part] = product(kv_ref[:, wide:], w2t)
        for member in range(members):
            drp_ref[member, :, part] = product(rkv_ref[member, :, wide:], w2t)
    for block in range(blocks):
        part = slice(block * BLOCK, (block + 1) * BLOCK)
        kt_ref[:, part] = kv_ref[part, :wide].astype(jnp.float32).T.astype(jnp.bfloat16)
        vt_ref[:, part] = kv_ref[part, wide:].astype(jnp.float32).T.astype(jnp.bfloat16)
    for member in range(members):
        rkt_ref[member] = rkv_ref[member, :, :wide].astype(jnp.float32).T.astype(jnp.bfloat16)
        rvt_ref[member] = rkv_ref[member, :, wide:].astype(jnp.float32).T.astype(jnp.bfloat16)
    gp_ref[...] = jnp.zeros_like(gp_ref)
    gr_ref[...] = jnp.zeros_like(gr_ref)
    reward_ref[...] = jnp.zeros_like(reward_ref)
    shades = [jnp.where(block < length, 0.0, -1e30) for block in range(blocks)]

    def step(index, carry):
        member = index // tiles
        tile = lax.rem(index, tiles)
        start = pl.multiple_of(tile * TILE, TILE)
        lane = pl.ds(pl.multiple_of(lax.rem(index, phases) * TILE, TILE), TILE)
        q = q_ref[member, pl.ds(start, TILE), :]
        first = mask_ref[lane, :]
        q2 = jnp.concatenate([q * first, q * (1 - first)], axis=1)
        s_ref[:span] = product_nt(kv_ref[:, :wide], q2)
        sr = product_nt(rkv_ref[member, :, :wide], q2)
        causal = (
            lax.broadcasted_iota(jnp.int32, (positions, TILE), 0) * heads
            <= lax.broadcasted_iota(jnp.int32, (positions, TILE), 1) + start
        )
        sr = jnp.where(causal, sr, -1e30)
        highest = jnp.max(sr, axis=0, keepdims=True)
        for block in range(blocks):
            part = slice(block * BLOCK, (block + 1) * BLOCK)
            top = jnp.max(s_ref[part, :], axis=0, keepdims=True) + shades[block]
            highest = jnp.maximum(highest, top)
        er = jnp.exp2((sr - highest) * pace)
        total = jnp.sum(er, axis=0, keepdims=True)
        for block in range(blocks):
            part = slice(block * BLOCK, (block + 1) * BLOCK)
            e = jnp.exp2((s_ref[part, :] - (highest - shades[block])) * pace)
            s_ref[part, :] = e
            total = total + jnp.sum(e, axis=0, keepdims=True)
        inverse = 1.0 / total
        pr = er * inverse
        lr = pr.astype(jnp.bfloat16)
        for block in range(blocks):
            part = slice(block * BLOCK, (block + 1) * BLOCK)
            p = s_ref[part, :] * inverse
            s_ref[part, :] = p
            p_ref[part, :] = p.astype(jnp.bfloat16)
        both = product(vt_ref[...], p_ref[...]) + product(rvt_ref[member], lr)
        first_t = mask_t_ref[:, lane]
        out = jnp.where(first_t > 0.5, both[:hd], both[hd:]).astype(jnp.bfloat16)
        out = out.astype(jnp.float32)
        wt = wt_ref[:, lane]
        reward_ref[pl.ds(member, 1), :] += jnp.sum(out * wt, axis=0, keepdims=True)
        delta = jnp.sum(
            out * wt.astype(jnp.bfloat16).astype(jnp.float32), axis=0, keepdims=True
        )
        for block in range(blocks):
            part = slice(block * BLOCK, (block + 1) * BLOCK)
            ds_ref[part, :] = (s_ref[part, :] * (dp_ref[part, lane] - delta)).astype(jnp.bfloat16)
        dsr = (pr * (drp_ref[member, :, lane] - delta)).astype(jnp.bfloat16)
        both = product(kt_ref[...], ds_ref[...]) + product(rkt_ref[member], dsr)
        gq = jnp.where(first_t > 0.5, both[:hd], both[hd:]) * scale
        gq_ref[member, pl.ds(start, TILE), :] = gq.T
        sign = (2 * member - 1).astype(jnp.float32).astype(jnp.bfloat16)
        w2 = w2_ref[lane, :]
        gr_ref[member, :, :wide] += product(dsr, q2)
        gr_ref[member, :, wide:] += product(lr, w2)
        gp_ref[:, :wide] += product(ds_ref[...], q2 * sign)
        gp_ref[:, wide:] += product(p_ref[...], w2 * sign)
        return carry

    lax.fori_loop(0, members * tiles, step, 0)
    gp_ref[:, :wide] = gp_ref[:, :wide] * scale
    gr_ref[:, :, :wide] = gr_ref[:, :, :wide] * scale


def attend(length, q, kv, rkv, w):
    members, rows, hd = q.shape
    span = kv.shape[0]
    positions = rkv.shape[1]
    heads = w.shape[0]
    period = heads * TILE // math.gcd(heads, TILE)
    wide = 2 * hd
    vmem = pl.BlockSpec(memory_space=pltpu.VMEM)
    return pl.pallas_call(
        attend_kernel,
        out_shape=(
            jax.ShapeDtypeStruct((members, rows, hd), jnp.float32),
            jax.ShapeDtypeStruct((span, 2 * wide), jnp.float32),
            jax.ShapeDtypeStruct((members, positions, 2 * wide), jnp.float32),
            jax.ShapeDtypeStruct((members, TILE), jnp.float32),
        ),
        in_specs=[pl.BlockSpec(memory_space=pltpu.SMEM)] + [vmem] * 4,
        out_specs=(vmem,) * 4,
        scratch_shapes=[
            pltpu.VMEM((period, hd), jnp.float32),
            pltpu.VMEM((hd, period), jnp.float32),
            pltpu.VMEM((period, hd), jnp.bfloat16),
            pltpu.VMEM((hd, period), jnp.float32),
            pltpu.VMEM((period, wide), jnp.bfloat16),
            pltpu.VMEM((wide, span), jnp.bfloat16),
            pltpu.VMEM((wide, span), jnp.bfloat16),
            pltpu.VMEM((members, wide, positions), jnp.bfloat16),
            pltpu.VMEM((members, wide, positions), jnp.bfloat16),
            pltpu.VMEM((span, period), jnp.float32),
            pltpu.VMEM((members, positions, period), jnp.float32),
            pltpu.VMEM((span, TILE), jnp.float32),
            pltpu.VMEM((span, TILE), jnp.bfloat16),
            pltpu.VMEM((span, TILE), jnp.bfloat16),
        ],
        compiler_params=pltpu.CompilerParams(vmem_limit_bytes=48 * 2**20),
    )(length, q, kv, rkv, w)


def pack(kv):
    return jnp.swapaxes(kv, -3, -2).reshape(kv.shape[:-3] + (-1,))


def unpack(flat, kv_heads):
    hd = flat.shape[-1] // (2 * kv_heads)
    return jnp.swapaxes(flat.reshape(flat.shape[:-1] + (2, kv_heads, hd)), -3, -2)


def shards(queries, resp_kv, prompt_kv, prompt_of, prompt_len, reward_head):
    n_resp = lax.axis_size("resp")
    n_prompt = lax.axis_size("prompt")
    pair_index = lax.axis_index(("prompt", "resp"))
    resp_index = lax.axis_index("resp")
    prompt_id = prompt_of[pair_index]
    table = prompt_of.reshape(n_prompt, n_resp)
    column = lax.dynamic_index_in_dim(table, resp_index, 1, keepdims=False)
    length = prompt_len[prompt_id]
    _, members, positions, heads, hd = queries.shape
    kv_heads = prompt_kv.shape[2]

    own = pack(prompt_kv)
    every_prompt = lax.all_gather(own, "resp", axis=0, tiled=True)
    picked = jnp.take(every_prompt, column, axis=0)
    arrived = lax.all_to_all(picked, "prompt", split_axis=0, concat_axis=0, tiled=True)
    whole = arrived.reshape(-1, arrived.shape[-1])

    q = queries.reshape(members, positions * heads, hd)
    gq, gp, gr, reward = attend(length[None], q, whole, pack(resp_kv[0]), reward_head)
    reward = lax.psum(jnp.sum(reward, axis=1), "tensor") / positions
    margin = reward[1] - reward[0]
    pair_loss = jnp.logaddexp(0.0, margin)
    gain = jax.nn.sigmoid(margin) * (loss_scale / positions)
    gains = jnp.stack([-gain, gain])
    query_out = (gq * gains[:, None, None]).astype(jnp.bfloat16).reshape(queries.shape)
    resp_out = unpack((gr * gains[:, None, None]).astype(jnp.bfloat16), kv_heads)[None]

    pieces = (gp * gain).astype(jnp.bfloat16).reshape(arrived.shape)
    returned = lax.all_to_all(pieces, "prompt", split_axis=0, concat_axis=0, tiled=True)
    selector = (column[:, None] == jnp.arange(n_resp)[None, :]).astype(jnp.float32)
    dense = jnp.einsum(
        "pn,prj->nrj",
        selector,
        returned.astype(jnp.float32),
        precision=lax.Precision.HIGHEST,
    )
    owned = lax.psum_scatter(dense.astype(jnp.bfloat16), "resp", scatter_dimension=0, tiled=True)
    return (pair_loss[None], query_out, resp_out, unpack(owned, kv_heads))


def solution(mesh):
    in_specs = (
        P(("prompt", "resp"), None, None, "tensor", None),
        P(("prompt", "resp"), None, None, "tensor", None, None),
        P("resp", "prompt", "tensor", None, None),
        P(),
        P(),
        P("tensor", None),
    )
    out_specs = (
        P(("prompt", "resp")),
        P(("prompt", "resp"), None, None, "tensor", None),
        P(("prompt", "resp"), None, None, "tensor", None, None),
        P("resp", "prompt", "tensor", None, None),
    )
    return jax.shard_map(shards, mesh=mesh, in_specs=in_specs, out_specs=out_specs, check_vma=False)
```

time: 381 us -> 347 us (0.911)
  matrix products: 37.5 us -> 0.91 us
  Pallas kernels: 0 us -> 23.9 us
  other arithmetic: 22 us -> 3.68 us
  local copies, waits for them, and re-layouts: 25.5 us -> 14.4 us
  waiting for transfers between devices: 231 us -> 241 us
    pallas_call x0 -> x1, Pallas kernels: none -> 23.9 us  [attend(): pl.pallas_call(attend_kernel, out_shape=(jax.ShapeDtypeStruct((members, r...]
    dot_general x25 -> x1, matrix products: 22.5 us -> 0.91 us  [shards(): jnp.einsum('pn,prj->nrj', selector, returned.astype(jnp.float32), precisi...]
    sub x4 -> x0, matrix products: 15 us -> none  [block_probs(): exponent = jnp.exp(scores - highest)]
    reduce_scatter x1, waiting for transfers between devices: 110 us -> 119 us  [shards(): lax.psum_scatter(dense.astype(jnp.bfloat16), 'resp', scatter_dimension=0,...]
    unnamed x124 -> x18, local copies, waits for them, and re-layouts: 12.9 us -> 4.51 us
    reduce_sum x5 -> x1, other arithmetic: 8.12 us -> 0.12 us  [shards(): reward = lax.psum(jnp.sum(reward, axis=1), 'tensor') / positions]
    another operation x5 -> x1, other arithmetic: 5.23 us -> 0.08 us  [shards(): gains = jnp.stack([-gain, gain])]
  transfers between devices with their start and end apart: 3 -> 3, of which waited for: 3 -> 3; matrix products, arithmetic and copies ran while one was open for 4% -> 1% of each run, Pallas kernels for 0% -> 0%
where the time goes in v1:
time: 347 us
  waiting for transfers between devices  241 us (69%)
  blocking collectives  38.6 us (11%)
  Pallas kernels  23.9 us (7%)
  between operations  18.7 us (5%)
  local copies, waits for them, and re-layouts  14.4 us (4%)
  starting transfers between devices  4.93 us (1%)
  other arithmetic  3.68 us (1%)
    reduce_scatter x1, waiting for transfers between devices, shards(): lax.psum_scatter(dense.astype(jnp.bfloat16), 'resp', scatter_dimension=0,...  119 us
    all_gather x1, waiting for transfers between devices, shards(): every_prompt = lax.all_gather(own, 'resp', axis=0, tiled=True)  100 us
    all_to_all x1, blocking collectives, shards(): lax.all_to_all(pieces, 'prompt', split_axis=0, concat_axis=0, tiled=True)  30.9 us
    pallas_call x1, Pallas kernels, attend(): pl.pallas_call(attend_kernel, out_shape=(jax.ShapeDtypeStruct((members, r...  23.9 us
    all_to_all x1, waiting for transfers between devices, shards(): lax.all_to_all(picked, 'prompt', split_axis=0, concat_axis=0, tiled=True)  22.4 us
    psum x1, blocking collectives, shards(): reward = lax.psum(jnp.sum(reward, axis=1), 'tensor') / positions  7.73 us
  transfers between devices with their start and end apart: 3, of which 3 were waited for; matrix products, arithmetic and copies ran while one was open for 1% of the time, Pallas kernels for 0%

profile of v1, /device:TPU:1, one launch (start us, length us, event | category | flops | bytes accessed | tf_op | source)
XLA Modules:
  0.0 346.6 jit_solution(15478758197557121095)
XLA Ops:
  7.2 0.0 all-gather.2.cloned.1.call-start
  7.2 1.0 copy.21
  8.2 0.8 copy.22
  9.0 0.0 all-gather.2.cloned.1.call-update
  9.1 0.7 reshape.42
  9.8 0.7 dynamic-slice_reduce_fusion
  10.5 0.2 and_reduce_fusion
  10.7 100.4 %all-gather.2.cloned.1.call-done = bf16[16,128,512]{2,1,0:T(8,128)(2,1)} async-done(((bf16[1,128,512]{2,1,0:T(8,128)(2,1)}), bf16[16,128,512]{2,1,0:T(8,128)(2,1)}) %all-gather.2.cloned.1.call-update) | async-done | bytes 2097168 | tf_op jit(solution)/shard_map/all_gather | solution.py:216
  111.1 2.2 gather_fusion
  113.3 0.0 copy-start.6
  113.3 0.0 copy-start.4
  113.3 0.0 copy-start.7
  113.3 0.0 copy-start.3
  113.3 1.1 broadcast_select_fusion
  114.5 4.9 %all-to-all-start = ((bf16[8,128,512]{2,1,0:T(8,128)(2,1)}), bf16[8,128,512]{2,1,0:T(8,128)(2,1)S(1)}, u32[]{:S(2)}, u32[]{:S(2)}) async-start(bf16[8,128,512]{2,1,0:T(8,128)(2,1)} %broadcast_select_fusion), calls=%async_computation | async-start | bytes 2097152 | tf_op jit(solution)/shard_map/all_to_all | solution.py:218
  119.4 0.0 reduce-scatter.2.cloned.1.call-start
  119.4 0.0 copy-done.6
  119.4 0.6 dynamic_slice.10
  121.3 0.0 copy-done.4
  121.3 0.1 copy.23
  121.4 0.1 reshape.45.rkv_ref
  122.1 0.0 copy-done.7
  122.1 0.6 dynamic_slice.11.length_ref
  122.7 22.4 %all-to-all-done = bf16[8,128,512]{2,1,0:T(8,128)(2,1)S(1)} async-done(((bf16[8,128,512]{2,1,0:T(8,128)(2,1)}), bf16[8,128,512]{2,1,0:T(8,128)(2,1)S(1)}, u32[]{:S(2)}, u32[]{:S(2)}) %all-to-all-start) | async-done | bytes 1048608 | tf_op jit(solution)/shard_map/all_to_all | solution.py:218
  145.1 0.0 copy-done.3
  145.1 0.0 copy-start.2
  145.1 1.1 copy-done.2
  146.3 23.9 %shard_map.93 = (f32[2,1536,128]{2,1,0:T(8,128)S(1)}, f32[1024,512]{1,0:T(8,128)S(1)}, f32[2,64,512]{2,1,0:T(8,128)S(1)}, f32[2,256]{1,0:T(2,128)S(1)}) custom-call(s32[1]{0:T(128)} %dynamic_slice.11.length_ref, bf16[2,1536,128]{2,1,0:T(8,128)(2,1)S(1)} %bitcast.27, bf16[1024,512]{1,0:T(8,128)(2,1)S(1)} %bitcast.26, ...), custom_call_target="tpu_custom_call" | custom-call | tf_op jit(solution)/shard_map/pallas_call | solution.py:164
  170.2 0.0 copy-start
  170.2 1.1 copy-done
  171.3 0.1 reduce_sum.9
  171.5 7.7 %psum.7 = f32[2]{0:T(128)S(1)} all-reduce(f32[2]{0:T(128)S(1)} %reduce_sum.9), channel_id=1, replica_groups=mesh['prompt'=8,'resp'=16,'tensor'=4] {'tensor'}, use_global_device_ids=true, to_apply=%region_1.2 | all-reduce | flops 2 | bytes 16 | tf_op jit(solution)/shard_map/psum | solution.py:223
  179.2 0.6 fusion.5
  181.2 0.0 copy-start.5
  181.2 0.3 multiply_convert_fusion
  181.5 30.9 %all_to_all.10 = bf16[8,128,512]{2,1,0:T(8,128)(2,1)S(1)} all-to-all(bf16[8,128,512]{2,1,0:T(8,128)(2,1)S(1)} %bitcast.28), channel_id=1, replica_groups=mesh['prompt'=8,'resp'=16,'tensor'=4] {'prompt'}, dimensions={0} | all-to-all | bytes 2097152 | tf_op jit(solution)/shard_map/all_to_all | solution.py:232
  212.3 0.0 copy-done.5
  212.3 0.9 convolution_convert_fusion
  213.2 2.5 copy.26
  215.8 0.0 copy-start.1
  215.8 0.0 reduce-scatter.2.cloned.1.call-update
  215.9 0.1 pad_maximum_fusion
  216.0 0.1 multiply_convert_fusion.2
  216.1 0.7 copy.32
  216.8 0.4 copy-done.1
  217.2 1.1 multiply_convert_fusion.1
  218.3 118.5 %reduce-scatter.2.cloned.1.call-done = bf16[1,128,512]{2,1,0:T(8,128)(2,1)} async-done(((bf16[16,128,512]{2,1,0:T(8,128)(2,1)}), bf16[1,128,512]{2,1,0:T(8,128)(2,1)}) %reduce-scatter.2.cloned.1.call-update) | async-done | bytes 131088 | tf_op jit(solution)/shard_map/reduce_scatter | solution.py:240
  336.8 1.0 copy.27
  337.8 0.8 copy.28
  (3 shorter events, 0.0 us)
Async XLA Ops:
  7.2 103.9 %all-gather.2.cloned.1.call-start = ((), (), s32[]{:S(2)}) async-start(), calls=%async_computation.3 | async-start | bytes 2228224 | tf_op jit(solution)/shard_map/all_gather | solution.py:216
  113.3 6.1 %copy-start.6 = (s32[128]{0:T(128)S(1)}, s32[128]{0:T(128)}, u32[]{:S(2)}) copy-start(s32[128]{0:T(128)} %param.9) | copy-start | bytes 1540
  113.3 8.0 %copy-start.4 = (bf16[1,2,64,2,2,128]{5,4,3,2,1,0:T(2,128)(2,1)S(1)}, bf16[1,2,64,2,2,128]{5,4,3,2,1,0:T(2,128)(2,1)}, u32[]{:S(2)}) copy-start(bf16[1,2,64,2,2,128]{5,4,3,2,1,0:T(2,128)(2,1)} %param.7) | copy-start | bytes 393220
  113.3 8.8 %copy-start.7 = (s32[16]{0:T(128)S(1)}, s32[16]{0:T(128)}, u32[]{:S(2)}) copy-start(s32[16]{0:T(128)} %param.10) | copy-start | bytes 196
  113.3 31.8 %copy-start.3 = (f32[24,128]{1,0:T(8,128)S(1)}, f32[24,128]{1,0:T(8,128)}, u32[]{:S(2)}) copy-start(f32[24,128]{1,0:T(8,128)} %w_ref.1) | copy-start | bytes 36868
  114.5 30.6 %all-to-all-start = ((bf16[8,128,512]{2,1,0:T(8,128)(2,1)}), bf16[8,128,512]{2,1,0:T(8,128)(2,1)S(1)}, u32[]{:S(2)}, u32[]{:S(2)}) async-start(bf16[8,128,512]{2,1,0:T(8,128)(2,1)} %broadcast_select_fusion), calls=%async_computation | async-start | bytes 2097152 | tf_op jit(solution)/shard_map/all_to_all | solution.py:218
  119.4 217.4 %reduce-scatter.2.cloned.1.call-start = ((), (), s32[]{:S(2)}) async-start(), calls=%async_computation.4 | async-start | bytes 2228224 | tf_op jit(solution)/shard_map/reduce_scatter | solution.py:240
  145.1 1.1 copy-start.2
  170.2 1.1 copy-start
  181.2 31.2 %copy-start.5 = (s32[8]{0:T(128)S(1)}, s32[8]{0:T(128)}, u32[]{:S(2)}) copy-start(s32[8]{0:T(128)} %get-tuple-element.20) | copy-start | bytes 100
  215.8 1.5 copy-start.1
Sparse Core Ops, SparseCore 0:
  11.6 99.4 all-gather.1
  215.9 120.8 reduce-scatter.1

commit v2 on v1

--- a/solution.py
+++ b/solution.py
@@ -191,6 +191,309 @@
     )(length, q, kv, rkv, w)
 
 
+LONG = 4
+WIDE = 4
+MESH = pl.DeviceIdType.MESH
+
+
+class Place:
+    def __init__(self):
+        prompt = lax.axis_index("prompt")
+        resp = lax.axis_index("resp")
+        self.core = lax.rem(prompt, 2)
+        self.low = lax.div(prompt, 2)
+        self.high = lax.div(resp, WIDE)
+        self.x = lax.rem(resp, WIDE)
+        self.tensor = lax.axis_index("tensor")
+        self.z = self.high * LONG + self.low
+
+    def at(self, dz, dx, core):
+        ring = LONG * LONG
+        z = lax.rem(self.z + dz + ring, ring)
+        x = lax.rem(self.x + dx + WIDE, WIDE)
+        return (lax.rem(z, LONG) * 2 + core, lax.div(z, LONG) * WIDE + x, self.tensor)
+
+    def block(self, dz, core):
+        return lax.rem(self.low + dz + LONG, LONG) * 2 + core
+
+
+def remote(src, dst, send, recv, target):
+    return pltpu.make_async_remote_copy(
+        src_ref=src,
+        dst_ref=dst,
+        send_sem=send,
+        recv_sem=recv,
+        device_id=target,
+        device_id_type=MESH,
+    )
+
+
+def greet(senders):
+    barrier = pltpu.get_barrier_semaphore()
+    for device in senders:
+        pl.semaphore_signal(barrier, inc=1, device_id=device, device_id_type=MESH)
+    pl.semaphore_wait(barrier, len(senders))
+
+
+def gather_kernel(prompt_of_ref, own_ref, whole_ref, all_ref, out_ref, z_send, z_recv, x_send, x_recv, c_send, c_recv):
+    me = Place()
+    core = me.core
+    rows = own_ref.shape[0]
+    half = rows // 2
+    parts = (pl.ds(0, half), pl.ds(half, half))
+    up, down = me.at(LONG, 0, core), me.at(-LONG, 0, core)
+    right, left = me.at(0, 1, core), me.at(0, -1, core)
+    greet(
+        [up, down, right, left, me.at(0, 0, 1 - core), me.at(-2, 0, 0), me.at(2, 0, 1)]
+        + [me.at(dz, 0, c) for dz in (1, -1) for c in range(2)]
+    )
+
+    def slot(dzh, dx):
+        return lax.rem(me.high + dzh + LONG, LONG) * WIDE + lax.rem(me.x + dx + WIDE, WIDE)
+
+    sent = []
+
+    def push(ref, sends, recvs, index, target):
+        copy = remote(ref, ref, sends.at[index], recvs.at[index], target)
+        copy.start()
+        sent.append(copy)
+
+    def await_copy(ref, recvs, index):
+        remote(ref, ref, z_send.at[0], recvs.at[index], up).wait_recv()
+
+    def spread(order, dzh):
+        block = all_ref.at[slot(dzh, 0)]
+        push(block, x_send, x_recv, 4 * order, right)
+        push(block, x_send, x_recv, 4 * order + 1, left)
+
+    def relay(order, dzh):
+        block = all_ref.at[slot(dzh, -1)]
+        await_copy(block, x_recv, 4 * order)
+        push(block.at[parts[0]], x_send, x_recv, 4 * order + 2, right)
+        block = all_ref.at[slot(dzh, 1)]
+        await_copy(block, x_recv, 4 * order + 1)
+        push(block.at[parts[1]], x_send, x_recv, 4 * order + 3, left)
+
+    all_ref[slot(0, 0)] = own_ref[...]
+    block = all_ref.at[slot(0, 0)]
+    push(block, z_send, z_recv, 0, up)
+    push(block, z_send, z_recv, 1, down)
+    spread(0, 0)
+    block = all_ref.at[slot(-1, 0)]
+    await_copy(block, z_recv, 0)
+    push(block.at[parts[0]], z_send, z_recv, 2, up)
+    block = all_ref.at[slot(1, 0)]
+    await_copy(block, z_recv, 1)
+    push(block.at[parts[1]], z_send, z_recv, 3, down)
+    spread(1, -1)
+    spread(2, 1)
+    relay(0, 0)
+    block = all_ref.at[slot(2, 0)]
+    await_copy(block.at[parts[0]], z_recv, 2)
+    await_copy(block.at[parts[1]], z_recv, 3)
+    spread(3, 2)
+    for order, dzh in ((1, -1), (2, 1), (3, 2)):
+        relay(order, dzh)
+    for order, dzh in ((0, 0), (1, -1), (2, 1), (3, 2)):
+        block = all_ref.at[slot(dzh, 2)]
+        await_copy(block.at[parts[0]], x_recv, 4 * order + 2)
+        await_copy(block.at[parts[1]], x_recv, 4 * order + 3)
+
+    here = whole_ref.at[pl.ds(me.block(0, core) * rows, rows)]
+    n_resp = LONG * WIDE
+
+    def wanted(device):
+        return all_ref[prompt_of_ref[device[0] * n_resp + device[1]]]
+
+    far = 2 - 4 * core
+    index = 0
+    for kind, dz in ((3, far), (1, 1), (2, -1), (0, 0)):
+        for c in range(2) if kind else (1 - core,):
+            target = me.at(dz, 0, c)
+            out_ref[index] = wanted(target)
+            copy = remote(out_ref.at[index], here, c_send.at[index], c_recv.at[2 * kind + core], target)
+            copy.start()
+            sent.append(copy)
+            index += 1
+    here[...] = wanted(me.at(0, 0, core))
+    for kind, dz in ((0, 0), (1, -1), (2, 1), (3, 2)):
+        for c in range(2) if kind else (1 - core,):
+            block = whole_ref.at[pl.ds(me.block(dz, c) * rows, rows)]
+            remote(block, block, c_send.at[0], c_recv.at[2 * kind + c], up).wait_recv()
+    for copy in sent:
+        copy.wait_send()
+
+
+def gather(prompt_of, own):
+    rows, width = own.shape
+    n_prompt, n_resp = 2 * LONG, LONG * WIDE
+    vmem = pl.BlockSpec(memory_space=pltpu.VMEM)
+    dma = pltpu.SemaphoreType.DMA
+    return pl.pallas_call(
+        gather_kernel,
+        out_shape=jax.ShapeDtypeStruct((n_prompt * rows, width), own.dtype),
+        in_specs=[pl.BlockSpec(memory_space=pltpu.SMEM), vmem],
+        out_specs=vmem,
+        scratch_shapes=[
+            pltpu.VMEM((n_resp, rows, width), own.dtype),
+            pltpu.VMEM((n_prompt - 1, rows, width), own.dtype),
+            dma((4,)),
+            dma((4,)),
+            dma((16,)),
+            dma((16,)),
+            dma((n_prompt,)),
+            dma((n_prompt,)),
+        ],
+        compiler_params=pltpu.CompilerParams(
+            collective_id=0, has_side_effects=True, vmem_limit_bytes=32 * 2**20
+        ),
+    )(prompt_of, own)
+
+
+def scatter_kernel(prompt_of_ref, piece_ref, owned_ref, got_ref, dense_ref, sum_ref, x1_ref, x2_ref, z1_ref, z2_ref, z_send, z_recv, x_send, x_recv, c_send, c_recv):
+    me = Place()
+    core = me.core
+    rows, width = owned_ref.shape
+    half = rows // 2
+    parts = (pl.ds(0, half), pl.ds(half, half))
+    up, down = me.at(LONG, 0, core), me.at(-LONG, 0, core)
+    right, left = me.at(0, 1, core), me.at(0, -1, core)
+    far = 2 - 4 * core
+    n_resp = LONG * WIDE
+    greet(
+        [up, down, right, left, me.at(0, 0, 1 - core)]
+        + [me.at(dz, 0, c) for dz in (1, -1, far) for c in range(2)]
+    )
+
+    def add(left_ref, right_ref):
+        return left_ref[...].astype(jnp.float32) + right_ref[...].astype(jnp.float32)
+
+    sent = []
+
+    def push(src, dst, sends, recvs, index, landing, target):
+        copy = remote(src, dst, sends.at[index], recvs.at[landing], target)
+        copy.start()
+        sent.append(copy)
+
+    def await_copy(ref, recvs, index):
+        remote(ref, ref, z_send.at[0], recvs.at[index], up).wait_recv()
+
+    index = 0
+    for kind, dz in ((3, 2), (1, 1), (2, -1), (0, 0)):
+        for c in range(2) if kind else (1 - core,):
+            block = piece_ref.at[pl.ds(me.block(dz, c) * rows, rows)]
+            target = me.at(dz if kind != 3 else 4 * c - 2, 0, c)
+            push(block, got_ref.at[2 * kind + core], c_send, c_recv, index, 2 * kind + core, target)
+            index += 1
+    got_ref[core] = piece_ref[pl.ds(me.block(0, core) * rows, rows), :]
+    names = []
+    for kind, dz in ((0, 0), (1, -1), (2, 1), (3, far)):
+        for c in range(2):
+            device = me.at(dz, 0, c)
+            names.append(prompt_of_ref[device[0] * n_resp + device[1]])
+    for kind in range(4):
+        for c in range(2) if kind else (1 - core,):
+            await_copy(got_ref.at[2 * kind + c], c_recv, 2 * kind + c)
+
+    chunk = 16
+    strip = 128
+    for order, dzh in enumerate((2, 1, 3, 0)):
+        base = lax.rem(me.high + dzh, LONG) * WIDE
+        for dx in (2, 1, 3, 0):
+            prompt = base + lax.rem(me.x + dx, WIDE)
+            picks = [jnp.where(name == prompt, 1.0, 0.0) for name in names]
+
+            def select(index, carry):
+                row = pl.ds(pl.multiple_of(index * chunk, chunk), chunk)
+                for start in range(0, width, strip):
+                    column = slice(start, start + strip)
+                    total = picks[0] * got_ref[0, row, column].astype(jnp.float32)
+                    for source in range(1, len(names)):
+                        total += picks[source] * got_ref[source, row, column].astype(jnp.float32)
+                    dense_ref[dzh, dx, row, column] = total.astype(dense_ref.dtype)
+                return carry
+
+            lax.fori_loop(0, rows // chunk, select, 0)
+            if dx == 2:
+                block = dense_ref.at[dzh, dx]
+                push(block.at[parts[0]], x1_ref.at[0, dzh], x_send, x_recv, 4 * order, 4 * order, right)
+                push(block.at[parts[1]], x1_ref.at[1, dzh], x_send, x_recv, 4 * order + 1, 4 * order + 1, left)
+
+    def x_turn(order, dzh):
+        for side, (dx, target) in enumerate(((1, right), (3, left))):
+            landed = x1_ref.at[side, dzh]
+            await_copy(landed, x_recv, 4 * order + side)
+            block = dense_ref.at[dzh, dx]
+            section = block.at[parts[side]]
+            section[...] = add(section, landed).astype(section.dtype)
+            push(block, x2_ref.at[side, dzh], x_send, x_recv, 4 * order + 2 + side, 4 * order + 2 + side, target)
+
+    def x_end(order, dzh):
+        for side in range(2):
+            await_copy(x2_ref.at[side, dzh], x_recv, 4 * order + 2 + side)
+        total = add(x2_ref.at[0, dzh], x2_ref.at[1, dzh])
+        sum_ref[dzh] = (total + dense_ref[dzh, 0].astype(jnp.float32)).astype(sum_ref.dtype)
+
+    def z_turn(side, dzh, target):
+        landed = z1_ref.at[side]
+        await_copy(landed, z_recv, side)
+        block = sum_ref.at[dzh]
+        section = block.at[parts[side]]
+        section[...] = add(section, landed).astype(section.dtype)
+        push(block, z2_ref.at[side], z_send, z_recv, 2 + side, 2 + side, target)
+
+    x_turn(0, 2)
+    x_turn(1, 1)
+    x_turn(2, 3)
+    x_turn(3, 0)
+    x_end(0, 2)
+    push(sum_ref.at[2, parts[0]], z1_ref.at[0], z_send, z_recv, 0, 0, up)
+    push(sum_ref.at[2, parts[1]], z1_ref.at[1], z_send, z_recv, 1, 1, down)
+    x_end(1, 1)
+    z_turn(0, 1, up)
+    x_end(2, 3)
+    z_turn(1, 3, down)
+    x_end(3, 0)
+    for side in range(2):
+        await_copy(z2_ref.at[side], z_recv, 2 + side)
+    total = add(z2_ref.at[0], z2_ref.at[1]) + sum_ref[0].astype(jnp.float32)
+    owned_ref[...] = total.astype(owned_ref.dtype)
+    for copy in sent:
+        copy.wait_send()
+
+
+def scatter(prompt_of, pieces):
+    n_prompt, n_resp = 2 * LONG, LONG * WIDE
+    rows, width = pieces.shape[0] // n_prompt, pieces.shape[1]
+    vmem = pl.BlockSpec(memory_space=pltpu.VMEM)
+    dma = pltpu.SemaphoreType.DMA
+    dtype = pieces.dtype
+    return pl.pallas_call(
+        scatter_kernel,
+        out_shape=jax.ShapeDtypeStruct((rows, width), dtype),
+        in_specs=[pl.BlockSpec(memory_space=pltpu.SMEM), vmem],
+        out_specs=vmem,
+        scratch_shapes=[
+            pltpu.VMEM((n_prompt, rows, width), dtype),
+            pltpu.VMEM((LONG, WIDE, rows, width), dtype),
+            pltpu.VMEM((LONG, rows, width), dtype),
+            pltpu.VMEM((2, LONG, rows // 2, width), dtype),
+            pltpu.VMEM((2, LONG, rows, width), dtype),
+            pltpu.VMEM((2, rows // 2, width), dtype),
+            pltpu.VMEM((2, rows, width), dtype),
+            dma((4,)),
+            dma((4,)),
+            dma((16,)),
+            dma((16,)),
+            dma((n_prompt,)),
+            dma((n_prompt,)),
+        ],
+        compiler_params=pltpu.CompilerParams(
+            collective_id=1, has_side_effects=True, vmem_limit_bytes=32 * 2**20
+        ),
+    )(prompt_of, pieces)
+
+
 def pack(kv):
     return jnp.swapaxes(kv, -3, -2).reshape(kv.shape[:-3] + (-1,))
 
@@ -201,22 +504,12 @@
 
 
 def shards(queries, resp_kv, prompt_kv, prompt_of, prompt_len, reward_head):
-    n_resp = lax.axis_size("resp")
-    n_prompt = lax.axis_size("prompt")
     pair_index = lax.axis_index(("prompt", "resp"))
-    resp_index = lax.axis_index("resp")
-    prompt_id = prompt_of[pair_index]
-    table = prompt_of.reshape(n_prompt, n_resp)
-    column = lax.dynamic_index_in_dim(table, resp_index, 1, keepdims=False)
-    length = prompt_len[prompt_id]
+    length = prompt_len[prompt_of[pair_index]]
     _, members, positions, heads, hd = queries.shape
     kv_heads = prompt_kv.shape[2]
 
-    own = pack(prompt_kv)
-    every_prompt = lax.all_gather(own, "resp", axis=0, tiled=True)
-    picked = jnp.take(every_prompt, column, axis=0)
-    arrived = lax.all_to_all(picked, "prompt", split_axis=0, concat_axis=0, tiled=True)
-    whole = arrived.reshape(-1, arrived.shape[-1])
+    whole = gather(prompt_of, pack(prompt_kv[0]))
 
     q = queries.reshape(members, positions * heads, hd)
     gq, gp, gr, reward = attend(length[None], q, whole, pack(resp_kv[0]), reward_head)
@@ -228,17 +521,8 @@
     query_out = (gq * gains[:, None, None]).astype(jnp.bfloat16).reshape(queries.shape)
     resp_out = unpack((gr * gains[:, None, None]).astype(jnp.bfloat16), kv_heads)[None]
 
-    pieces = (gp * gain).astype(jnp.bfloat16).reshape(arrived.shape)
-    returned = lax.all_to_all(pieces, "prompt", split_axis=0, concat_axis=0, tiled=True)
-    selector = (column[:, None] == jnp.arange(n_resp)[None, :]).astype(jnp.float32)
-    dense = jnp.einsum(
-        "pn,prj->nrj",
-        selector,
-        returned.astype(jnp.float32),
-        precision=lax.Precision.HIGHEST,
-    )
-    owned = lax.psum_scatter(dense.astype(jnp.bfloat16), "resp", scatter_dimension=0, tiled=True)
-    return (pair_loss[None], query_out, resp_out, unpack(owned, kv_heads))
+    owned = scatter(prompt_of, (gp * gain).astype(jnp.bfloat16))
+    return (pair_loss[None], query_out, resp_out, unpack(owned, kv_heads)[None])
 
 
 def solution(mesh):

time: 347 us -> 158 us (0.46)
  waiting for transfers between devices: 241 us -> 0 us
  Pallas kernels: 23.9 us -> 132 us
  blocking collectives: 38.6 us -> 8.74 us
  between operations: 18.7 us -> 5.31 us
  local copies, waits for them, and re-layouts: 14.4 us -> 8.63 us
  starting transfers between devices: 4.93 us -> 0 us
    reduce_scatter x1 -> x0, waiting for transfers between devices: 119 us -> none  [shards(): lax.psum_scatter(dense.astype(jnp.bfloat16), 'resp', scatter_dimension=0,...]
    pallas_call x0 -> x2, Pallas kernels: none -> 108 us  [the longest x1 60.2 us: gather(): pl.pallas_call(gather_kernel, out_shape=jax.ShapeDtypeStruct((n_prompt *...]
    all_gather x1 -> x0, waiting for transfers between devices: 100 us -> none  [shards(): every_prompt = lax.all_gather(own, 'resp', axis=0, tiled=True)]
    all_to_all x1 -> x0, blocking collectives: 30.9 us -> none  [shards(): lax.all_to_all(pieces, 'prompt', split_axis=0, concat_axis=0, tiled=True)]
    all_to_all x1 -> x0, waiting for transfers between devices: 22.4 us -> none  [shards(): lax.all_to_all(picked, 'prompt', split_axis=0, concat_axis=0, tiled=True)]
    all_to_all x1 -> x0, starting transfers between devices: 4.89 us -> none  [shards(): lax.all_to_all(picked, 'prompt', split_axis=0, concat_axis=0, tiled=True)]
  transfers between devices with their start and end apart: 3 -> 0, of which waited for: 3 -> 0; matrix products, arithmetic and copies ran while one was open for 1% -> 0% of each run, Pallas kernels for 0% -> 0%
where the time goes in v2:
time: 158 us; the launch traced here: 156 us
  Pallas kernels  132 us (84%)
  blocking collectives  8.74 us (6%)
  local copies, waits for them, and re-layouts  8.63 us (5%)
  between operations  5.31 us (3%)
  other arithmetic  1.63 us (1%)
    pallas_call x1, Pallas kernels, gather(): pl.pallas_call(gather_kernel, out_shape=jax.ShapeDtypeStruct((n_prompt *...  60.2 us
    pallas_call x1, Pallas kernels, scatter(): pl.pallas_call(scatter_kernel, out_shape=jax.ShapeDtypeStruct((rows, widt...  47.8 us
    pallas_call x1, Pallas kernels, attend(): pl.pallas_call(attend_kernel, out_shape=(jax.ShapeDtypeStruct((members, r...  23.8 us
    psum x1, blocking collectives, shards(): reward = lax.psum(jnp.sum(reward, axis=1), 'tensor') / positions  8.74 us

profile of v2, /device:TPU:1, one launch (start us, length us, event | category | flops | bytes accessed | tf_op | source)
XLA Modules:
  0.0 156.1 jit_solution(11020899871147889820)
XLA Ops:
  0.6 0.0 copy-start.3
  0.6 0.0 copy-start.2
  0.7 1.3 dynamic_slice.6
  3.9 1.2 dynamic_slice.7.length_ref
  5.2 1.0 copy.11
  6.1 0.1 reshape.30.rkv_ref
  6.2 1.0 copy.10
  7.2 0.1 reshape.29.own_ref
  7.3 0.0 copy-start.4
  7.3 0.6 copy-done.4
  7.9 60.2 %shard_map.93.kv_ref = bf16[1024,512]{1,0:T(8,128)(2,1)S(1)} custom-call(s32[128]{0:T(128)S(1)} %copy-done.4, bf16[128,512]{1,0:T(8,128)(2,1)S(1)} %reshape.29.own_ref), custom_call_target="tpu_custom_call" | custom-call | tf_op jit(solution)/shard_map/pallas_call | solution.py:332
  68.2 0.0 copy-done.3
  68.2 0.0 copy-done.2
  68.2 23.8 %shard_map.94 = (f32[2,1536,128]{2,1,0:T(8,128)S(1)}, f32[1024,512]{1,0:T(8,128)S(1)}, f32[2,64,512]{2,1,0:T(8,128)S(1)}, f32[2,256]{1,0:T(2,128)S(1)}) custom-call(s32[1]{0:T(128)} %dynamic_slice.7.length_ref, bf16[2,1536,128]{2,1,0:T(8,128)(2,1)S(1)} %bitcast.23, bf16[1024,512]{1,0:T(8,128)(2,1)S(1)} %shard_map.93.kv_ref, ...), custom_call_target="tpu_custom_call" | custom-call | tf_op jit(solution)/shard_map/pallas_call | solution.py:164
  92.0 0.0 copy-start
  92.0 1.2 copy-done
  93.1 0.0 copy-start.5
  93.1 0.1 reduce_sum.9
  93.2 8.7 %psum.7 = f32[2]{0:T(128)S(1)} all-reduce(f32[2]{0:T(128)S(1)} %reduce_sum.9), channel_id=1, replica_groups=mesh['prompt'=8,'resp'=16,'tensor'=4] {'tensor'}, use_global_device_ids=true, to_apply=%region_1.0 | all-reduce | flops 2 | bytes 16 | tf_op jit(solution)/shard_map/psum | solution.py:516
  102.0 0.6 fusion
  104.1 0.0 copy-start.1
  104.1 0.3 multiply_convert_fusion.piece_ref
  104.3 0.0 copy-done.5
  104.4 47.8 %shard_map.95 = bf16[128,512]{1,0:T(8,128)(2,1)S(1)} custom-call(s32[128]{0:T(128)S(1)} %copy-done.5, bf16[1024,512]{1,0:T(8,128)(2,1)S(1)} %multiply_convert_fusion.piece_ref), custom_call_target="tpu_custom_call" | custom-call | tf_op jit(solution)/shard_map/pallas_call | solution.py:471
  152.1 0.1 pad_maximum_fusion
  152.2 0.0 copy-done.1
  152.2 1.1 multiply_convert_fusion.1
  153.3 0.1 multiply_convert_fusion.2
  153.4 0.7 copy.17
  154.2 0.7 copy.16
  (3 shorter events, 0.1 us)
Async XLA Ops:
  0.6 67.5 %copy-start.3 = (f32[24,128]{1,0:T(8,128)S(1)}, f32[24,128]{1,0:T(8,128)}, u32[]{:S(2)}) copy-start(f32[24,128]{1,0:T(8,128)} %w_ref.1) | copy-start | bytes 36868
  0.6 67.5 %copy-start.2 = (bf16[1,2,64,24,128]{4,3,2,1,0:T(8,128)(2,1)S(1)}, bf16[1,2,64,24,128]{4,3,2,1,0:T(8,128)(2,1)}, u32[]{:S(2)}) copy-start(bf16[1,2,64,24,128]{4,3,2,1,0:T(8,128)(2,1)} %param.6) | copy-start | bytes 2359300
  7.3 0.7 copy-start.4
  92.0 1.2 copy-start
  93.1 11.2 %copy-start.5 = (s32[128]{0:T(128)S(1)}, s32[128]{0:T(128)}, u32[]{:S(2)}) copy-start(s32[128]{0:T(128)} %prompt_of_ref.3) | copy-start | bytes 1540
  104.1 48.2 %copy-start.1 = (f32[2,1536,128]{2,1,0:T(8,128)S(1)}, f32[2,1536,128]{2,1,0:T(8,128)}, u32[]{:S(2)}) copy-start(f32[2,1536,128]{2,1,0:T(8,128)} %copy-done) | copy-start | bytes 4718596

commit v3 on v1

v3 whole, which is shorter than its diff:
```python
import math

import jax
import jax.numpy as jnp
from jax import lax
from jax.experimental import pallas as pl
from jax.experimental.pallas import tpu as pltpu
from jax.sharding import PartitionSpec as P

BLOCK = 128
TILE = 256

loss_scale = 8192.0


def product(left, right):
    return jnp.dot(left, right, preferred_element_type=jnp.float32)


def product_nt(left, right):
    return lax.dot_general(
        left, right, (((1,), (1,)), ((), ())), preferred_element_type=jnp.float32
    )


LONG = 4
WIDE = 4
MESH = pl.DeviceIdType.MESH


class Place:
    def __init__(self):
        prompt = lax.axis_index("prompt")
        resp = lax.axis_index("resp")
        self.core = lax.rem(prompt, 2)
        self.low = lax.div(prompt, 2)
        self.high = lax.div(resp, WIDE)
        self.x = lax.rem(resp, WIDE)
        self.tensor = lax.axis_index("tensor")
        self.z = self.high * LONG + self.low

    def at(self, dz, dx, core):
        ring = LONG * LONG
        z = lax.rem(self.z + dz + ring, ring)
        x = lax.rem(self.x + dx + WIDE, WIDE)
        return (lax.rem(z, LONG) * 2 + core, lax.div(z, LONG) * WIDE + x, self.tensor)

    def block(self, dz, core):
        return lax.rem(self.low + dz + LONG, LONG) * 2 + core


def remote(src, dst, send, recv, target):
    return pltpu.make_async_remote_copy(
        src_ref=src,
        dst_ref=dst,
        send_sem=send,
        recv_sem=recv,
        device_id=target,
        device_id_type=MESH,
    )


def pair_kernel(
    prompt_of_ref,
    prompt_len_ref,
    q_ref,
    own_ref,
    rkv_ref,
    w_ref,
    gq_ref,
    gr_ref,
    owned_ref,
    margin_ref,
    all_k_ref,
    all_v_ref,
    out_ref,
    whole_ref,
    wrow_ref,
    wt_ref,
    mask_ref,
    mask_t_ref,
    w2_ref,
    w2t_ref,
    kt_ref,
    vt_ref,
    rkt_ref,
    rvt_ref,
    dp_ref,
    drp_ref,
    p_ref,
    pr_ref,
    low_ref,
    delta_ref,
    reward_ref,
    gqf_ref,
    gpf_ref,
    grf_ref,
    vote_ref,
    piece_ref,
    got_ref,
    dense_ref,
    sum_ref,
    x1_ref,
    x2_ref,
    z1_ref,
    z2_ref,
    z_send,
    z_recv,
    x_send,
    x_recv,
    c_send,
    c_recv,
    y_send,
    y_recv,
    zb_send,
    zb_recv,
    xb_send,
    xb_recv,
    cb_send,
    cb_recv,
):
    members, rows, hd = q_ref.shape
    block_rows = own_ref.shape[1]
    span = whole_ref.shape[1]
    positions = rkv_ref.shape[2]
    heads = w_ref.shape[0]
    blocks = span // BLOCK
    period = wrow_ref.shape[0]
    phases = period // TILE
    tiles = rows // TILE
    wide = 2 * hd
    scale = hd**-0.5
    pace = scale * math.log2(math.e)
    n_resp = LONG * WIDE
    n_tensor = vote_ref.shape[0]

    me = Place()
    core = me.core
    half = block_rows // 2
    parts = (pl.ds(0, half), pl.ds(half, half))
    up, down = me.at(LONG, 0, core), me.at(-LONG, 0, core)
    right, left = me.at(0, 1, core), me.at(0, -1, core)
    far = 2 - 4 * core
    here = me.at(0, 0, core)
    peers = [
        (here[0], here[1], lax.rem(me.tensor + step, n_tensor)) for step in range(1, n_tensor)
    ]
    barrier = pltpu.get_barrier_semaphore()
    friends = (
        [up, down, right, left, me.at(0, 0, 1 - core)]
        + [me.at(dz, 0, c) for dz in (1, -1) for c in range(2)]
        + [me.at(-2, 0, 0), me.at(2, 0, 1), me.at(far, 0, core)]
        + peers
    )
    for device in friends:
        pl.semaphore_signal(barrier, inc=1, device_id=device, device_id_type=MESH)
    pl.semaphore_wait(barrier, len(friends))

    sent = []

    def push(src, dst, send, recv, target):
        copy = remote(src, dst, send, recv, target)
        copy.start()
        sent.append(copy)

    def landed(ref, recv):
        remote(ref, ref, y_send.at[0], recv, up).wait_recv()

    def slot(dzh, dx):
        return lax.rem(me.high + dzh + LONG, LONG) * WIDE + lax.rem(me.x + dx + WIDE, WIDE)

    tables = (all_k_ref, all_v_ref)

    def spread(part, order, dzh):
        block = tables[part].at[slot(dzh, 0)]
        for side, target in enumerate((right, left)):
            index = 4 * order + side
            push(block, block, x_send.at[part, index], x_recv.at[part, index], target)

    def relay(part, order, dzh):
        for side, (dx, target) in enumerate(((-1, right), (1, left))):
            block = tables[part].at[slot(dzh, dx)]
            landed(block, x_recv.at[part, 4 * order + side])
            section = block.at[parts[side]]
            index = 4 * order + 2 + side
            push(section, section, x_send.at[part, index], x_recv.at[part, index], target)

    def begin(part):
        tables[part][slot(0, 0)] = own_ref[part]
        block = tables[part].at[slot(0, 0)]
        push(block, block, z_send.at[part, 0], z_recv.at[part, 0], up)
        push(block, block, z_send.at[part, 1], z_recv.at[part, 1], down)
        spread(part, 0, 0)

    def turn(part):
        for side, (dzh, target) in enumerate(((-1, up), (1, down))):
            block = tables[part].at[slot(dzh, 0)]
            landed(block, z_recv.at[part, side])
            section = block.at[parts[side]]
            push(section, section, z_send.at[part, 2 + side], z_recv.at[part, 2 + side], target)

    def finish(part):
        spread(part, 1, -1)
        spread(part, 2, 1)
        relay(part, 0, 0)
        block = tables[part].at[slot(2, 0)]
        for side in range(2):
            landed(block.at[parts[side]], z_recv.at[part, 2 + side])
        spread(part, 3, 2)
        for order, dzh in ((1, -1), (2, 1), (3, 2)):
            relay(part, order, dzh)
        for order, dzh in ((0, 0), (1, -1), (2, 1), (3, 2)):
            block = tables[part].at[slot(dzh, 2)]
            for side in range(2):
                landed(block.at[parts[side]], x_recv.at[part, 4 * order + 2 + side])

    def place(device_block):
        return pl.ds(pl.multiple_of(device_block * block_rows, block_rows), block_rows)

    def name(device):
        return prompt_of_ref[device[0] * n_resp + device[1]]

    def deliver(part):
        mine = whole_ref.at[part, place(me.block(0, core))]
        index = 0
        for kind, dz in ((3, far), (1, 1), (2, -1), (0, 0)):
            for c in range(2) if kind else (1 - core,):
                target = me.at(dz, 0, c)
                out_ref[part, index] = tables[part][name(target)]
                push(
                    out_ref.at[part, index],
                    mine,
                    c_send.at[part, index],
                    c_recv.at[part, 2 * kind + core],
                    target,
                )
                index += 1
        mine[...] = tables[part][name(here)]

    def receive(part):
        for kind, dz in ((0, 0), (1, -1), (2, 1), (3, 2)):
            for c in range(2) if kind else (1 - core,):
                landed(whole_ref.at[part, place(me.block(dz, c))], c_recv.at[part, 2 * kind + c])

    begin(0)

    for index in range(period // heads):
        wrow_ref[index * heads : (index + 1) * heads, :] = w_ref[...]
    for phase in range(phases):
        part = slice(phase * TILE, (phase + 1) * TILE)
        row = lax.broadcasted_iota(jnp.int32, (TILE, hd), 0) + phase * TILE
        first = (lax.rem(row, heads) < heads // 2).astype(jnp.float32)
        wrow = wrow_ref[part, :]
        mask_ref[part, :] = first.astype(jnp.bfloat16)
        mask_t_ref[:, part] = first.T
        wt_ref[:, part] = wrow.T
        w2 = jnp.concatenate([wrow * first, wrow * (1.0 - first)], axis=1)
        w2_ref[part, :] = w2.astype(jnp.bfloat16)
        w2t_ref[:, part] = w2.T.astype(jnp.bfloat16)
    for member in range(members):
        rkt_ref[member] = rkv_ref[member, 0].astype(jnp.float32).T.astype(jnp.bfloat16)
        rvt_ref[member] = rkv_ref[member, 1].astype(jnp.float32).T.astype(jnp.bfloat16)
        drp_ref[member] = product(rkv_ref[member, 1], w2t_ref[...])
    gpf_ref[...] = jnp.zeros_like(gpf_ref)
    grf_ref[...] = jnp.zeros_like(grf_ref)
    reward_ref[...] = jnp.zeros_like(reward_ref)

    turn(0)
    begin(1)
    finish(0)
    deliver(0)
    turn(1)
    finish(1)
    deliver(1)

    length = prompt_len_ref[name(here)]
    shades = [jnp.where(block < length, 0.0, -1e30) for block in range(blocks)]
    strips = [slice(block * BLOCK, (block + 1) * BLOCK) for block in range(blocks)]

    def where_is(index):
        member = lax.div(index, tiles)
        start = pl.multiple_of(lax.rem(index, tiles) * TILE, TILE)
        lane = pl.ds(pl.multiple_of(lax.rem(index, phases) * TILE, TILE), TILE)
        sign = (2 * member - 1).astype(jnp.float32).astype(jnp.bfloat16)
        return member, start, lane, sign

    def stacked(member, start, lane):
        q = q_ref[member, pl.ds(start, TILE), :]
        first = mask_ref[lane, :]
        return jnp.concatenate([q * first, q * (1 - first)], axis=1)

    def score_step(index, carry):
        member, start, lane, sign = where_is(index)
        q2 = stacked(member, start, lane)
        p_ref[index] = product_nt(whole_ref[0], q2)
        sr = product_nt(rkv_ref[member, 0], q2)
        causal = (
            lax.broadcasted_iota(jnp.int32, (positions, TILE), 0) * heads
            <= lax.broadcasted_iota(jnp.int32, (positions, TILE), 1) + start
        )
        sr = jnp.where(causal, sr, -1e30)
        highest = jnp.max(sr, axis=0, keepdims=True)
        for strip, shade in zip(strips, shades):
            top = jnp.max(p_ref[index, strip, :], axis=0, keepdims=True) + shade
            highest = jnp.maximum(highest, top)
        er = jnp.exp2((sr - highest) * pace)
        total = jnp.sum(er, axis=0, keepdims=True)
        for strip, shade in zip(strips, shades):
            e = jnp.exp2((p_ref[index, strip, :] - (highest - shade)) * pace)
            p_ref[index, strip, :] = e
            total = total + jnp.sum(e, axis=0, keepdims=True)
        inverse = 1.0 / total
        pr = er * inverse
        pr_ref[index] = pr
        for strip in strips:
            p = p_ref[index, strip, :] * inverse
            p_ref[index, strip, :] = p
            low_ref[index, strip, :] = p.astype(jnp.bfloat16)
        w2 = w2_ref[lane, :]
        grf_ref[member, 1] += product(pr.astype(jnp.bfloat16), w2)
        gpf_ref[1] += product(low_ref[index], w2 * sign)
        return carry

    def out_step(index, carry):
        member, start, lane, sign = where_is(index)
        both = product(vt_ref[...], low_ref[index])
        both += product(rvt_ref[member], pr_ref[index].astype(jnp.bfloat16))
        out = jnp.where(mask_t_ref[:, lane] > 0.5, both[:hd], both[hd:]).astype(jnp.bfloat16)
        out = out.astype(jnp.float32)
        wt = wt_ref[:, lane]
        reward_ref[pl.ds(member, 1), :] += jnp.sum(out * wt, axis=0, keepdims=True)
        delta_ref[pl.ds(index, 1), :] = jnp.sum(
            out * wt.astype(jnp.bfloat16).astype(jnp.float32), axis=0, keepdims=True
        )
        return carry

    def back_step(index, carry):
        member, start, lane, sign = where_is(index)
        q2 = stacked(member, start, lane)
        delta = delta_ref[pl.ds(index, 1), :]
        for strip in strips:
            low_ref[index, strip, :] = (
                p_ref[index, strip, :] * (dp_ref[strip, lane] - delta)
            ).astype(jnp.bfloat16)
        dsr = (pr_ref[index] * (drp_ref[member, :, lane] - delta)).astype(jnp.bfloat16)
        both = product(kt_ref[...], low_ref[index]) + product(rkt_ref[member], dsr)
        gq = jnp.where(mask_t_ref[:, lane] > 0.5, both[:hd], both[hd:]) * scale
        gqf_ref[member, pl.ds(start, TILE), :] = gq.T
        grf_ref[member, 0] += product(dsr, q2)
        gpf_ref[0] += product(low_ref[index], q2 * sign)
        return carry

    count = members * tiles
    receive(0)
    for strip in strips:
        kt_ref[:, strip] = whole_ref[0, strip, :].astype(jnp.float32).T.astype(jnp.bfloat16)
    lax.fori_loop(0, count, score_step, 0)
    receive(1)
    for strip in strips:
        vt_ref[:, strip] = whole_ref[1, strip, :].astype(jnp.float32).T.astype(jnp.bfloat16)
    lax.fori_loop(0, count, out_step, 0)

    ballot = vote_ref.at[me.tensor]
    for member in range(members):
        total = jnp.sum(reward_ref[member : member + 1, :], axis=1, keepdims=True)
        ballot[8 * member : 8 * (member + 1), :] = jnp.broadcast_to(total, (8, hd))
    for step, target in enumerate(peers):
        push(ballot, ballot, y_send.at[step], y_recv.at[step], target)
    dp_ref[...] = product(whole_ref[1], w2t_ref[...])
    lax.fori_loop(0, count // 2, back_step, 0)

    for step in range(1, n_tensor):
        source = lax.rem(me.tensor + n_tensor - step, n_tensor)
        landed(vote_ref.at[source], y_recv.at[step - 1])
    reward = vote_ref[0]
    for index in range(1, n_tensor):
        reward = reward + vote_ref[index]
    reward = reward / positions
    margin = reward[8:16] - reward[:8]
    margin_ref[...] = margin
    tiny = jnp.exp(-jnp.abs(margin))
    sigmoid_gap = jnp.where(margin >= 0.0, 1.0, tiny) / (1.0 + tiny)
    gain = sigmoid_gap[:1] * (loss_scale / positions)
    gain2 = jnp.concatenate([gain, gain], axis=1)

    def give(part):
        factor = gain2 if part else gain2 * scale
        for strip in strips:
            piece_ref[part, strip, :] = (gpf_ref[part, strip, :] * factor).astype(jnp.bfloat16)
        index = 0
        for kind, dz in ((3, 2), (1, 1), (2, -1), (0, 0)):
            for c in range(2) if kind else (1 - core,):
                target = me.at(dz if kind != 3 else 4 * c - 2, 0, c)
                push(
                    piece_ref.at[part, place(me.block(dz, c))],
                    got_ref.at[part, 2 * kind + core],
                    cb_send.at[part, index],
                    cb_recv.at[part, 2 * kind + core],
                    target,
                )
                index += 1
        got_ref[part, core] = piece_ref[part, place(me.block(0, core)), :]

    names = [
        name(me.at(dz, 0, c)) for kind, dz in ((0, 0), (1, -1), (2, 1), (3, far)) for c in range(2)
    ]
    chunk = 16
    lanes = 128
    turns = (2, 1, 3, 0)

    def add(left_ref, right_ref):
        return left_ref[...].astype(jnp.float32) + right_ref[...].astype(jnp.float32)

    def collect(part):
        for kind in range(4):
            for c in range(2) if kind else (1 - core,):
                landed(got_ref.at[part, 2 * kind + c], cb_recv.at[part, 2 * kind + c])
        for order, dzh in enumerate(turns):
            base = lax.rem(me.high + dzh, LONG) * WIDE
            for dx in turns:
                prompt = base + lax.rem(me.x + dx, WIDE)
                picks = [jnp.where(each == prompt, 1.0, 0.0) for each in names]

                def select(index, carry):
                    row = pl.ds(pl.multiple_of(index * chunk, chunk), chunk)
                    for start in range(0, wide, lanes):
                        column = slice(start, start + lanes)
                        total = picks[0] * got_ref[part, 0, row, column].astype(jnp.float32)
                        for source in range(1, len(names)):
                            total += picks[source] * got_ref[part, source, row, column].astype(
                                jnp.float32
                            )
                        dense_ref[part, dzh, dx, row, column] = total.astype(jnp.bfloat16)
                    return carry

                lax.fori_loop(0, block_rows // chunk, select, 0)
                if dx == 2:
                    for side, target in enumerate((right, left)):
                        push(
                            dense_ref.at[part, dzh, dx, parts[side]],
                            x1_ref.at[part, side, dzh],
                            xb_send.at[part, 4 * order + side],
                            xb_recv.at[part, 4 * order + side],
                            target,
                        )

    def x_turn(part, order):
        dzh = turns[order]
        for side, (dx, target) in enumerate(((1, right), (3, left))):
            arrival = x1_ref.at[part, side, dzh]
            landed(arrival, xb_recv.at[part, 4 * order + side])
            block = dense_ref.at[part, dzh, dx]
            section = block.at[parts[side]]
            section[...] = add(section, arrival).astype(jnp.bfloat16)
            index = 4 * order + 2 + side
            push(
                block,
                x2_ref.at[part, side, dzh],
                xb_send.at[part, index],
                xb_recv.at[part, index],
                target,
            )

    def x_end(part, order):
        dzh = turns[order]
        for side in range(2):
            landed(x2_ref.at[part, side, dzh], xb_recv.at[part, 4 * order + 2 + side])
        total = add(x2_ref.at[part, 0, dzh], x2_ref.at[part, 1, dzh])
        total += dense_ref[part, dzh, 0].astype(jnp.float32)
        sum_ref[part, dzh] = total.astype(jnp.bfloat16)

    def z_begin(part):
        for side, target in enumerate((up, down)):
            push(
                sum_ref.at[part, 2, parts[side]],
                z1_ref.at[part, side],
                zb_send.at[part, side],
                zb_recv.at[part, side],
                target,
            )

    def z_turn(part):
        for side, (dzh, target) in enumerate(((1, up), (3, down))):
            arrival = z1_ref.at[part, side]
            landed(arrival, zb_recv.at[part, side])
            block = sum_ref.at[part, dzh]
            section = block.at[parts[side]]
            section[...] = add(section, arrival).astype(jnp.bfloat16)
            push(
                block,
                z2_ref.at[part, side],
                zb_send.at[part, 2 + side],
                zb_recv.at[part, 2 + side],
                target,
            )

    def z_end(part):
        for side in range(2):
            landed(z2_ref.at[part, side], zb_recv.at[part, 2 + side])
        total = add(z2_ref.at[part, 0], z2_ref.at[part, 1])
        total += sum_ref[part, 0].astype(jnp.float32)
        owned_ref[part] = total.astype(jnp.bfloat16)

    give(1)
    lax.fori_loop(count // 2, count, back_step, 0)
    give(0)
    collect(1)
    for order in range(LONG):
        x_turn(1, order)
    x_end(1, 0)
    z_begin(1)
    collect(0)
    x_end(1, 1)
    x_end(1, 2)
    z_turn(1)
    x_end(1, 3)
    for order in range(LONG):
        x_turn(0, order)
    x_end(0, 0)
    z_begin(0)

    def write_step(index, carry):
        member, start, lane, sign = where_is(index)
        factor = gain * (2 * member - 1).astype(jnp.float32)
        part = pl.ds(start, TILE)
        gq_ref[member, part, :] = (gqf_ref[member, part, :] * factor).astype(jnp.bfloat16)
        return carry

    lax.fori_loop(0, count, write_step, 0)
    for member in range(members):
        factor = gain2 if member else -gain2
        gr_ref[member, 0] = (grf_ref[member, 0] * (factor * scale)).astype(jnp.bfloat16)
        gr_ref[member, 1] = (grf_ref[member, 1] * factor).astype(jnp.bfloat16)

    x_end(0, 1)
    x_end(0, 2)
    z_turn(0)
    x_end(0, 3)
    z_end(1)
    z_end(0)
    for copy in sent:
        copy.wait_send()


def pair_call(prompt_of, prompt_len, q, own, rkv, w, n_tensor):
    members, rows, hd = q.shape
    _, block_rows, wide = own.shape
    positions = rkv.shape[2]
    heads = w.shape[0]
    n_prompt, n_resp = 2 * LONG, LONG * WIDE
    span = n_prompt * block_rows
    period = heads * TILE // math.gcd(heads, TILE)
    count = members * rows // TILE
    half = block_rows // 2
    vmem = pl.BlockSpec(memory_space=pltpu.VMEM)
    smem = pl.BlockSpec(memory_space=pltpu.SMEM)
    dma = pltpu.SemaphoreType.DMA
    low, full = jnp.bfloat16, jnp.float32

    def ways():
        return [dma((2, 4)), dma((2, 4)), dma((2, 16)), dma((2, 16)), dma((2, 8)), dma((2, 8))]

    return pl.pallas_call(
        pair_kernel,
        out_shape=(
            jax.ShapeDtypeStruct((members, rows, hd), low),
            jax.ShapeDtypeStruct((members, 2, positions, wide), low),
            jax.ShapeDtypeStruct((2, block_rows, wide), low),
            jax.ShapeDtypeStruct((8, hd), full),
        ),
        in_specs=[smem] * 2 + [vmem] * 4,
        out_specs=(vmem,) * 4,
        scratch_shapes=[
            pltpu.VMEM((n_resp, block_rows, wide), low),
            pltpu.VMEM((n_resp, block_rows, wide), low),
            pltpu.VMEM((2, n_prompt - 1, block_rows, wide), low),
            pltpu.VMEM((2, span, wide), low),
            pltpu.VMEM((period, hd), full),
            pltpu.VMEM((hd, period), full),
            pltpu.VMEM((period, hd), low),
            pltpu.VMEM((hd, period), full),
            pltpu.VMEM((period, wide), low),
            pltpu.VMEM((wide, period), low),
            pltpu.VMEM((wide, span), low),
            pltpu.VMEM((wide, span), low),
            pltpu.VMEM((members, wide, positions), low),
            pltpu.VMEM((members, wide, positions), low),
            pltpu.VMEM((span, period), full),
            pltpu.VMEM((members, positions, period), full),
            pltpu.VMEM((count, span, TILE), full),
            pltpu.VMEM((count, positions, TILE), full),
            pltpu.VMEM((count, span, TILE), low),
            pltpu.VMEM((16, TILE), full),
            pltpu.VMEM((8, TILE), full),
            pltpu.VMEM((members, rows, hd), full),
            pltpu.VMEM((2, span, wide), full),
            pltpu.VMEM((members, 2, positions, wide), full),
            pltpu.VMEM((n_tensor, 8 * members, hd), full),
            pltpu.VMEM((2, span, wide), low),
            pltpu.VMEM((2, n_prompt, block_rows, wide), low),
            pltpu.VMEM((2, LONG, WIDE, block_rows, wide), low),
            pltpu.VMEM((2, LONG, block_rows, wide), low),
            pltpu.VMEM((2, 2, LONG, half, wide), low),
            pltpu.VMEM((2, 2, LONG, block_rows, wide), low),
            pltpu.VMEM((2, 2, half, wide), low),
            pltpu.VMEM((2, 2, block_rows, wide), low),
            *ways(),
            dma((n_tensor - 1,)),
            dma((n_tensor - 1,)),
            *ways(),
        ],
        compiler_params=pltpu.CompilerParams(
            collective_id=0, has_side_effects=True, vmem_limit_bytes=56 * 2**20
        ),
    )(prompt_of, prompt_len, q, own, rkv, w)


def pack(kv):
    flat = jnp.moveaxis(kv, -2, -4)
    return flat.reshape(flat.shape[:-2] + (-1,))


def unpack(flat, kv_heads):
    split = flat.reshape(flat.shape[:-1] + (kv_heads, -1))
    return jnp.moveaxis(split, -4, -2)


def shards(queries, resp_kv, prompt_kv, prompt_of, prompt_len, reward_head):
    _, members, positions, heads, hd = queries.shape
    kv_heads = prompt_kv.shape[2]
    q = queries.reshape(members, positions * heads, hd)
    gq, gr, owned, margin = pair_call(
        prompt_of,
        prompt_len,
        q,
        pack(prompt_kv[0]),
        pack(resp_kv[0]),
        reward_head,
        lax.axis_size("tensor"),
    )
    pair_loss = jnp.logaddexp(0.0, margin[0, :1])
    return (
        pair_loss,
        gq.reshape(queries.shape),
        unpack(gr, kv_heads)[None],
        unpack(owned, kv_heads)[None],
    )


def solution(mesh):
    in_specs = (
        P(("prompt", "resp"), None, None, "tensor", None),
        P(("prompt", "resp"), None, None, "tensor", None, None),
        P("resp", "prompt", "tensor", None, None),
        P(),
        P(),
        P("tensor", None),
    )
    out_specs = (
        P(("prompt", "resp")),
        P(("prompt", "resp"), None, None, "tensor", None),
        P(("prompt", "resp"), None, None, "tensor", None, None),
        P("resp", "prompt", "tensor", None, None),
    )
    return jax.shard_map(shards, mesh=mesh, in_specs=in_specs, out_specs=out_specs, check_vma=False)
```

time: 347 us -> 132 us (0.38)
  the two profiles are of different devices: /device:TPU:1 before, /device:TPU:24 now
where the time goes in v3:
time: 132 us; the launch traced here: 131 us
  Pallas kernels  119 us (90%)
  local copies, waits for them, and re-layouts  8.43 us (6%)
  between operations  3.83 us (3%)
    pallas_call x1, Pallas kernels, pair_call(): pl.pallas_call(pair_kernel, out_shape=(jax.ShapeDtypeStruct((members, row...  119 us
    reshape x4, local copies, waits for them, and re-layouts, unpack(): split = flat.reshape(flat.shape[:-1] + (kv_heads, -1))  3.6 us

profile of v3, /device:TPU:24, one launch (start us, length us, event | category | flops | bytes accessed | tf_op | source)
XLA Modules:
  0.0 131.4 jit_solution(6214471205175166227)
XLA Ops:
  0.6 1.0 copy.11
  1.6 0.0 copy-start.1
  1.6 0.7 reshape.28.rkv_ref
  2.4 0.1 copy-done.1
  2.5 0.1 copy.10
  2.6 0.7 reshape.27.own_ref
  3.3 119.1 %shard_map.93 = (bf16[2,1536,128]{2,1,0:T(8,128)(2,1)}, bf16[2,2,64,256]{3,2,1,0:T(8,128)(2,1)}, bf16[2,128,256]{2,1,0:T(8,128)(2,1)}, f32[8,128]{1,0:T(8,128)}) custom-call(s32[128]{0:T(128)} %prompt_of_ref.1, s32[16]{0:T(128)} %prompt_len_ref.1, bf16[2,1536,128]{2,1,0:T(8,128)(2,1)} %bitcast.21, bf16[2,128,256]{2,1,0:T(8,128)(2,1)} %reshape.27.own_ref, ...), custom_call_target="tpu_custom_call" | custom-call | tf_op jit(solution)/shard_map/pallas_call | solution.py:563
  122.4 0.0 copy-start
  122.5 1.3 slice.3
  125.7 0.9 reshape.30
  126.7 0.9 copy.17
  127.5 0.9 reshape.31
  128.5 0.9 copy.16
  129.3 0.0 copy-done
  129.4 0.9 copy.19
Async XLA Ops:
  1.6 0.9 copy-start.1
  122.4 6.9 %copy-start = (bf16[2,1536,128]{2,1,0:T(8,128)(2,1)S(1)}, bf16[2,1536,128]{2,1,0:T(8,128)(2,1)}, u32[]{:S(2)}) copy-start(bf16[2,1536,128]{2,1,0:T(8,128)(2,1)} %get-tuple-element.9) | copy-start | bytes 2359300

commit v4 on v3

--- a/solution.py
+++ b/solution.py
@@ -70,7 +70,7 @@
     gq_ref,
     gr_ref,
     owned_ref,
-    margin_ref,
+    loss_ref,
     all_k_ref,
     all_v_ref,
     out_ref,
@@ -81,25 +81,29 @@
     mask_t_ref,
     w2_ref,
     w2t_ref,
+    rk_ref,
+    rv_ref,
     kt_ref,
     vt_ref,
     rkt_ref,
     rvt_ref,
     dp_ref,
     drp_ref,
-    p_ref,
-    pr_ref,
     low_ref,
+    w2i_ref,
+    q2i_ref,
+    inverse_ref,
     delta_ref,
     reward_ref,
     gqf_ref,
-    gpf_ref,
-    grf_ref,
     vote_ref,
+    gain_ref,
+    factor_ref,
     piece_ref,
     got_ref,
     dense_ref,
     sum_ref,
+    grf_ref,
     x1_ref,
     x2_ref,
     z1_ref,
@@ -112,6 +116,8 @@
     c_recv,
     y_send,
     y_recv,
+    g_send,
+    g_recv,
     zb_send,
     zb_recv,
     xb_send,
@@ -120,9 +126,9 @@
     cb_recv,
 ):
     members, rows, hd = q_ref.shape
-    block_rows = own_ref.shape[1]
+    block_rows = own_ref.shape[0]
     span = whole_ref.shape[1]
-    positions = rkv_ref.shape[2]
+    positions = rkv_ref.shape[1]
     heads = w_ref.shape[0]
     blocks = span // BLOCK
     period = wrow_ref.shape[0]
@@ -133,6 +139,18 @@
     pace = scale * math.log2(math.e)
     n_resp = LONG * WIDE
     n_tensor = vote_ref.shape[0]
+    count = members * tiles
+    keys = pl.ds(0, span)
+    tail = pl.ds(span, positions)
+
+    def pick(flat, part):
+        lows = [slice((2 * g + part) * hd, (2 * g + part + 1) * hd) for g in range(2)]
+        return jnp.concatenate([flat[:, low] for low in lows], axis=1)
+
+    def unpick(ref, part, value):
+        for g in range(2):
+            low = (2 * g + part) * hd
+            ref[:, low : low + hd] = value[:, g * hd : (g + 1) * hd]
 
     me = Place()
     core = me.core
@@ -186,7 +204,7 @@
             push(section, section, x_send.at[part, index], x_recv.at[part, index], target)
 
     def begin(part):
-        tables[part][slot(0, 0)] = own_ref[part]
+        tables[part][slot(0, 0)] = pick(own_ref[...], part)
         block = tables[part].at[slot(0, 0)]
         push(block, block, z_send.at[part, 0], z_recv.at[part, 0], up)
         push(block, block, z_send.at[part, 1], z_recv.at[part, 1], down)
@@ -199,16 +217,22 @@
             section = block.at[parts[side]]
             push(section, section, z_send.at[part, 2 + side], z_recv.at[part, 2 + side], target)
 
-    def finish(part):
+    def middle(part):
         spread(part, 1, -1)
         spread(part, 2, 1)
         relay(part, 0, 0)
+
+    def opposite(part):
         block = tables[part].at[slot(2, 0)]
         for side in range(2):
             landed(block.at[parts[side]], z_recv.at[part, 2 + side])
         spread(part, 3, 2)
+
+    def relays(part):
         for order, dzh in ((1, -1), (2, 1), (3, 2)):
             relay(part, order, dzh)
+
+    def complete(part):
         for order, dzh in ((0, 0), (1, -1), (2, 1), (3, 2)):
             block = tables[part].at[slot(dzh, 2)]
             for side in range(2):
@@ -258,107 +282,160 @@
         w2_ref[part, :] = w2.astype(jnp.bfloat16)
         w2t_ref[:, part] = w2.T.astype(jnp.bfloat16)
     for member in range(members):
-        rkt_ref[member] = rkv_ref[member, 0].astype(jnp.float32).T.astype(jnp.bfloat16)
-        rvt_ref[member] = rkv_ref[member, 1].astype(jnp.float32).T.astype(jnp.bfloat16)
-        drp_ref[member] = product(rkv_ref[member, 1], w2t_ref[...])
-    gpf_ref[...] = jnp.zeros_like(gpf_ref)
-    grf_ref[...] = jnp.zeros_like(grf_ref)
+        rk_ref[member] = pick(rkv_ref[member], 0)
+        rv_ref[member] = pick(rkv_ref[member], 1)
+        rkt_ref[member] = rk_ref[member].astype(jnp.float32).T.astype(jnp.bfloat16)
+        rvt_ref[member] = rv_ref[member].astype(jnp.float32).T.astype(jnp.bfloat16)
+        drp_ref[member] = product(rv_ref[member], w2t_ref[...])
     reward_ref[...] = jnp.zeros_like(reward_ref)
 
     turn(0)
     begin(1)
-    finish(0)
+    middle(0)
+    opposite(0)
+    relays(0)
+    turn(1)
+    complete(0)
     deliver(0)
-    turn(1)
-    finish(1)
+    middle(1)
+    opposite(1)
+    relays(1)
+    complete(1)
     deliver(1)
 
     length = prompt_len_ref[name(here)]
     shades = [jnp.where(block < length, 0.0, -1e30) for block in range(blocks)]
     strips = [slice(block * BLOCK, (block + 1) * BLOCK) for block in range(blocks)]
+
+    PAIRED = 2
 
     def where_is(index):
         member = lax.div(index, tiles)
         start = pl.multiple_of(lax.rem(index, tiles) * TILE, TILE)
         lane = pl.ds(pl.multiple_of(lax.rem(index, phases) * TILE, TILE), TILE)
-        sign = (2 * member - 1).astype(jnp.float32).astype(jnp.bfloat16)
-        return member, start, lane, sign
-
-    def stacked(member, start, lane):
+        column = pl.ds(pl.multiple_of(index * TILE, TILE), TILE)
+        sign = (2 * member - 1).astype(jnp.float32)
+        return member, start, lane, column, sign
+
+    def paired(step):
+        def body(index, carry):
+            for sub in range(PAIRED):
+                step(index * PAIRED + sub)
+            return carry
+
+        return body
+
+    def run(step, first, last):
+        lax.fori_loop(first // PAIRED, last // PAIRED, paired(step), 0)
+
+    wider = 2 * BLOCK
+    broad = [slice(start, start + wider) for start in range(0, span, wider)]
+
+    def score_step(index):
+        member, start, lane, column, sign = where_is(index)
         q = q_ref[member, pl.ds(start, TILE), :]
         first = mask_ref[lane, :]
-        return jnp.concatenate([q * first, q * (1 - first)], axis=1)
-
-    def score_step(index, carry):
-        member, start, lane, sign = where_is(index)
-        q2 = stacked(member, start, lane)
-        p_ref[index] = product_nt(whole_ref[0], q2)
-        sr = product_nt(rkv_ref[member, 0], q2)
+        q2 = jnp.concatenate([q * first, q * (1 - first)], axis=1)
+        sr = product_nt(rk_ref[member], q2)
         causal = (
             lax.broadcasted_iota(jnp.int32, (positions, TILE), 0) * heads
             <= lax.broadcasted_iota(jnp.int32, (positions, TILE), 1) + start
         )
         sr = jnp.where(causal, sr, -1e30)
         highest = jnp.max(sr, axis=0, keepdims=True)
-        for strip, shade in zip(strips, shades):
-            top = jnp.max(p_ref[index, strip, :], axis=0, keepdims=True) + shade
-            highest = jnp.maximum(highest, top)
+        for number, part in enumerate(broad):
+            s = product_nt(whole_ref[0, part, :], q2)
+            for sub in range(2):
+                top = jnp.max(s[sub * BLOCK : (sub + 1) * BLOCK], axis=0, keepdims=True)
+                highest = jnp.maximum(highest, top + shades[2 * number + sub])
         er = jnp.exp2((sr - highest) * pace)
         total = jnp.sum(er, axis=0, keepdims=True)
-        for strip, shade in zip(strips, shades):
-            e = jnp.exp2((p_ref[index, strip, :] - (highest - shade)) * pace)
-            p_ref[index, strip, :] = e
-            total = total + jnp.sum(e, axis=0, keepdims=True)
+        low_ref[tail, column] = er.astype(jnp.bfloat16)
+        for number, part in enumerate(broad):
+            s = product_nt(whole_ref[0, part, :], q2)
+            for sub in range(2):
+                shifted = s[sub * BLOCK : (sub + 1) * BLOCK] - (highest - shades[2 * number + sub])
+                e = jnp.exp2(shifted * pace)
+                total = total + jnp.sum(e, axis=0, keepdims=True)
+                low_ref[strips[2 * number + sub], column] = e.astype(jnp.bfloat16)
         inverse = 1.0 / total
-        pr = er * inverse
-        pr_ref[index] = pr
-        for strip in strips:
-            p = p_ref[index, strip, :] * inverse
-            p_ref[index, strip, :] = p
-            low_ref[index, strip, :] = p.astype(jnp.bfloat16)
-        w2 = w2_ref[lane, :]
-        grf_ref[member, 1] += product(pr.astype(jnp.bfloat16), w2)
-        gpf_ref[1] += product(low_ref[index], w2 * sign)
-        return carry
-
-    def out_step(index, carry):
-        member, start, lane, sign = where_is(index)
-        both = product(vt_ref[...], low_ref[index])
-        both += product(rvt_ref[member], pr_ref[index].astype(jnp.bfloat16))
-        out = jnp.where(mask_t_ref[:, lane] > 0.5, both[:hd], both[hd:]).astype(jnp.bfloat16)
-        out = out.astype(jnp.float32)
+        inverse_ref[pl.ds(index, 1), :] = inverse
+        turned = jnp.broadcast_to(inverse * sign, (hd, TILE)).T
+        qi = q.astype(jnp.float32) * turned
+        wi = wrow_ref[lane, :].astype(jnp.bfloat16).astype(jnp.float32) * turned
+        firstf = first.astype(jnp.float32)
+        q2i_ref[column, :] = jnp.concatenate([qi * firstf, qi * (1 - firstf)], axis=1).astype(
+            jnp.bfloat16
+        )
+        w2i_ref[column, :] = jnp.concatenate([wi * firstf, wi * (1 - firstf)], axis=1).astype(
+            jnp.bfloat16
+        )
+
+    def out_step(index):
+        member, start, lane, column, sign = where_is(index)
+        both = product(vt_ref[...], low_ref[keys, column])
+        both += product(rvt_ref[member], low_ref[tail, column])
+        out = jnp.where(mask_t_ref[:, lane] > 0.5, both[:hd], both[hd:])
+        out = (out * inverse_ref[pl.ds(index, 1), :]).astype(jnp.bfloat16).astype(jnp.float32)
         wt = wt_ref[:, lane]
         reward_ref[pl.ds(member, 1), :] += jnp.sum(out * wt, axis=0, keepdims=True)
         delta_ref[pl.ds(index, 1), :] = jnp.sum(
             out * wt.astype(jnp.bfloat16).astype(jnp.float32), axis=0, keepdims=True
         )
-        return carry
-
-    def back_step(index, carry):
-        member, start, lane, sign = where_is(index)
-        q2 = stacked(member, start, lane)
+
+    def back_step(index):
+        member, start, lane, column, sign = where_is(index)
         delta = delta_ref[pl.ds(index, 1), :]
         for strip in strips:
-            low_ref[index, strip, :] = (
-                p_ref[index, strip, :] * (dp_ref[strip, lane] - delta)
-            ).astype(jnp.bfloat16)
-        dsr = (pr_ref[index] * (drp_ref[member, :, lane] - delta)).astype(jnp.bfloat16)
-        both = product(kt_ref[...], low_ref[index]) + product(rkt_ref[member], dsr)
-        gq = jnp.where(mask_t_ref[:, lane] > 0.5, both[:hd], both[hd:]) * scale
+            low_ref[strip, column] = low_ref[strip, column] * (dp_ref[strip, lane] - delta).astype(
+                jnp.bfloat16
+            )
+        dsr = low_ref[tail, column] * (drp_ref[member, :, lane] - delta).astype(jnp.bfloat16)
+        low_ref[tail, column] = dsr
+        both = product(kt_ref[...], low_ref[keys, column]) + product(rkt_ref[member], dsr)
+        gq = jnp.where(mask_t_ref[:, lane] > 0.5, both[:hd], both[hd:])
+        gq = gq * (inverse_ref[pl.ds(index, 1), :] * (sign * scale))
         gqf_ref[member, pl.ds(start, TILE), :] = gq.T
-        grf_ref[member, 0] += product(dsr, q2)
-        gpf_ref[0] += product(low_ref[index], q2 * sign)
-        return carry
-
-    count = members * tiles
+
+    def sums(part, left):
+        right_ref = (q2i_ref, w2i_ref)[part]
+        factor = 1.0 if part else scale
+        for strip in left:
+            value = product(low_ref[strip, :], right_ref[...]) * factor
+            piece_ref[part, strip, :] = value.astype(jnp.bfloat16)
+
+    def resp_sums(part):
+        right_ref = (q2i_ref, w2i_ref)[part]
+        factor = 1.0 if part else scale
+        for member in range(members):
+            column = slice(member * rows, (member + 1) * rows)
+            grf_ref[member, part] = product(low_ref[tail, column], right_ref[column, :]) * factor
+
+    def give(part):
+        index = 0
+        for kind, dz in ((3, 2), (1, 1), (2, -1), (0, 0)):
+            for c in range(2) if kind else (1 - core,):
+                push(
+                    piece_ref.at[part, place(me.block(dz, c))],
+                    got_ref.at[part, 2 * kind + core],
+                    cb_send.at[part, index],
+                    cb_recv.at[part, 2 * kind + core],
+                    me.at(dz if kind != 3 else 4 * c - 2, 0, c),
+                )
+                index += 1
+        got_ref[part, core] = piece_ref[part, place(me.block(0, core)), :]
+
+    halves = [slice(0, span // 2), slice(span // 2, span)]
     receive(0)
     for strip in strips:
         kt_ref[:, strip] = whole_ref[0, strip, :].astype(jnp.float32).T.astype(jnp.bfloat16)
-    lax.fori_loop(0, count, score_step, 0)
+    run(score_step, 0, count)
+    sums(1, halves)
     receive(1)
+    give(1)
     for strip in strips:
         vt_ref[:, strip] = whole_ref[1, strip, :].astype(jnp.float32).T.astype(jnp.bfloat16)
-    lax.fori_loop(0, count, out_step, 0)
+    run(out_step, 0, count)
 
     ballot = vote_ref.at[me.tensor]
     for member in range(members):
@@ -366,8 +443,9 @@
         ballot[8 * member : 8 * (member + 1), :] = jnp.broadcast_to(total, (8, hd))
     for step, target in enumerate(peers):
         push(ballot, ballot, y_send.at[step], y_recv.at[step], target)
+    resp_sums(1)
     dp_ref[...] = product(whole_ref[1], w2t_ref[...])
-    lax.fori_loop(0, count // 2, back_step, 0)
+    run(back_step, 0, 4)
 
     for step in range(1, n_tensor):
         source = lax.rem(me.tensor + n_tensor - step, n_tensor)
@@ -377,29 +455,23 @@
         reward = reward + vote_ref[index]
     reward = reward / positions
     margin = reward[8:16] - reward[:8]
-    margin_ref[...] = margin
     tiny = jnp.exp(-jnp.abs(margin))
+    loss = jnp.maximum(margin, 0.0) + jnp.log1p(tiny)
+    loss_ref[0] = loss[0, 0]
     sigmoid_gap = jnp.where(margin >= 0.0, 1.0, tiny) / (1.0 + tiny)
-    gain = sigmoid_gap[:1] * (loss_scale / positions)
-    gain2 = jnp.concatenate([gain, gain], axis=1)
-
-    def give(part):
-        factor = gain2 if part else gain2 * scale
-        for strip in strips:
-            piece_ref[part, strip, :] = (gpf_ref[part, strip, :] * factor).astype(jnp.bfloat16)
-        index = 0
-        for kind, dz in ((3, 2), (1, 1), (2, -1), (0, 0)):
-            for c in range(2) if kind else (1 - core,):
-                target = me.at(dz if kind != 3 else 4 * c - 2, 0, c)
-                push(
-                    piece_ref.at[part, place(me.block(dz, c))],
-                    got_ref.at[part, 2 * kind + core],
-                    cb_send.at[part, index],
-                    cb_recv.at[part, 2 * kind + core],
-                    target,
-                )
-                index += 1
-        got_ref[part, core] = piece_ref[part, place(me.block(0, core)), :]
+    gain = sigmoid_gap * (loss_scale / positions)
+    gain_ref[core] = gain
+    index = 0
+    for kind, dz in ((3, 2), (1, 1), (2, -1), (0, 0)):
+        for c in range(2) if kind else (1 - core,):
+            push(
+                gain_ref.at[core],
+                gain_ref.at[2 * kind + core],
+                g_send.at[index],
+                g_recv.at[2 * kind + core],
+                me.at(dz if kind != 3 else 4 * c - 2, 0, c),
+            )
+            index += 1
 
     names = [
         name(me.at(dz, 0, c)) for kind, dz in ((0, 0), (1, -1), (2, 1), (3, far)) for c in range(2)
@@ -407,6 +479,19 @@
     chunk = 16
     lanes = 128
     turns = (2, 1, 3, 0)
+    sources = len(names)
+
+    def factors():
+        for kind in range(4):
+            for c in range(2) if kind else (1 - core,):
+                landed(gain_ref.at[2 * kind + c], g_recv.at[2 * kind + c])
+        for a in range(LONG):
+            for b in range(WIDE):
+                prompt = slot(a, b)
+                for source in range(sources):
+                    row = (a * WIDE + b) * sources + source
+                    share = jnp.where(names[source] == prompt, 1.0, 0.0)
+                    factor_ref[row : row + 1, :] = gain_ref[source, :1, :] * share
 
     def add(left_ref, right_ref):
         return left_ref[...].astype(jnp.float32) + right_ref[...].astype(jnp.float32)
@@ -415,34 +500,35 @@
         for kind in range(4):
             for c in range(2) if kind else (1 - core,):
                 landed(got_ref.at[part, 2 * kind + c], cb_recv.at[part, 2 * kind + c])
+
+        def select(index, carry):
+            row = pl.ds(pl.multiple_of(index * chunk, chunk), chunk)
+            for start in range(0, wide, lanes):
+                column = slice(start, start + lanes)
+                terms = [
+                    got_ref[part, source, row, column].astype(jnp.float32)
+                    for source in range(sources)
+                ]
+                for a in range(LONG):
+                    for b in range(WIDE):
+                        base = (a * WIDE + b) * sources
+                        total = terms[0] * factor_ref[base : base + 1, :]
+                        for source in range(1, sources):
+                            at = base + source
+                            total += terms[source] * factor_ref[at : at + 1, :]
+                        dense_ref[part, a, b, row, column] = total.astype(jnp.bfloat16)
+            return carry
+
+        lax.fori_loop(0, block_rows // chunk, select, 0)
         for order, dzh in enumerate(turns):
-            base = lax.rem(me.high + dzh, LONG) * WIDE
-            for dx in turns:
-                prompt = base + lax.rem(me.x + dx, WIDE)
-                picks = [jnp.where(each == prompt, 1.0, 0.0) for each in names]
-
-                def select(index, carry):
-                    row = pl.ds(pl.multiple_of(index * chunk, chunk), chunk)
-                    for start in range(0, wide, lanes):
-                        column = slice(start, start + lanes)
-                        total = picks[0] * got_ref[part, 0, row, column].astype(jnp.float32)
-                        for source in range(1, len(names)):
-                            total += picks[source] * got_ref[part, source, row, column].astype(
-                                jnp.float32
-                            )
-                        dense_ref[part, dzh, dx, row, column] = total.astype(jnp.bfloat16)
-                    return carry
-
-                lax.fori_loop(0, block_rows // chunk, select, 0)
-                if dx == 2:
-                    for side, target in enumerate((right, left)):
-                        push(
-                            dense_ref.at[part, dzh, dx, parts[side]],
-                            x1_ref.at[part, side, dzh],
-                            xb_send.at[part, 4 * order + side],
-                            xb_recv.at[part, 4 * order + side],
-                            target,
-                        )
+            for side, target in enumerate((right, left)):
+                push(
+                    dense_ref.at[part, dzh, 2, parts[side]],
+                    x1_ref.at[part, side, dzh],
+                    xb_send.at[part, 4 * order + side],
+                    xb_recv.at[part, 4 * order + side],
+                    target,
+                )
 
     def x_turn(part, order):
         dzh = turns[order]
@@ -499,44 +585,47 @@
             landed(z2_ref.at[part, side], zb_recv.at[part, 2 + side])
         total = add(z2_ref.at[part, 0], z2_ref.at[part, 1])
         total += sum_ref[part, 0].astype(jnp.float32)
-        owned_ref[part] = total.astype(jnp.bfloat16)
-
-    give(1)
-    lax.fori_loop(count // 2, count, back_step, 0)
-    give(0)
+        unpick(owned_ref, part, total.astype(jnp.bfloat16))
+
+    run(back_step, 4, 8)
+    factors()
     collect(1)
+    run(back_step, 8, 10)
     for order in range(LONG):
         x_turn(1, order)
+    run(back_step, 10, 12)
+    sums(0, halves)
+    give(0)
     x_end(1, 0)
     z_begin(1)
-    collect(0)
     x_end(1, 1)
     x_end(1, 2)
     z_turn(1)
     x_end(1, 3)
+    resp_sums(0)
+
+    def write_step(index):
+        member, start, lane, column, sign = where_is(index)
+        part = pl.ds(start, TILE)
+        gq_ref[member, part, :] = (gqf_ref[member, part, :] * gain_ref[core, :1, :]).astype(
+            jnp.bfloat16
+        )
+
+    run(write_step, 0, count)
+    gain2 = jnp.concatenate([gain[:1], gain[:1]], axis=1)
+    for member in range(members):
+        for part in range(2):
+            unpick(gr_ref.at[member], part, (grf_ref[member, part] * gain2).astype(jnp.bfloat16))
+    collect(0)
+    z_end(1)
     for order in range(LONG):
         x_turn(0, order)
     x_end(0, 0)
     z_begin(0)
-
-    def write_step(index, carry):
-        member, start, lane, sign = where_is(index)
-        factor = gain * (2 * member - 1).astype(jnp.float32)
-        part = pl.ds(start, TILE)
-        gq_ref[member, part, :] = (gqf_ref[member, part, :] * factor).astype(jnp.bfloat16)
-        return carry
-
-    lax.fori_loop(0, count, write_step, 0)
-    for member in range(members):
-        factor = gain2 if member else -gain2
-        gr_ref[member, 0] = (grf_ref[member, 0] * (factor * scale)).astype(jnp.bfloat16)
-        gr_ref[member, 1] = (grf_ref[member, 1] * factor).astype(jnp.bfloat16)
-
     x_end(0, 1)
     x_end(0, 2)
     z_turn(0)
     x_end(0, 3)
-    z_end(1)
     z_end(0)
     for copy in sent:
         copy.wait_send()
@@ -544,8 +633,9 @@
 
 def pair_call(prompt_of, prompt_len, q, own, rkv, w, n_tensor):
     members, rows, hd = q.shape
-    _, block_rows, wide = own.shape
-    positions = rkv.shape[2]
+    block_rows = own.shape[0]
+    wide = own.shape[1] // 2
+    positions = rkv.shape[1]
     heads = w.shape[0]
     n_prompt, n_resp = 2 * LONG, LONG * WIDE
     span = n_prompt * block_rows
@@ -564,12 +654,12 @@
         pair_kernel,
         out_shape=(
             jax.ShapeDtypeStruct((members, rows, hd), low),
-            jax.ShapeDtypeStruct((members, 2, positions, wide), low),
-            jax.ShapeDtypeStruct((2, block_rows, wide), low),
-            jax.ShapeDtypeStruct((8, hd), full),
+            jax.ShapeDtypeStruct((members, positions, 2 * wide), low),
+            jax.ShapeDtypeStruct((block_rows, 2 * wide), low),
+            jax.ShapeDtypeStruct((1,), full),
         ),
         in_specs=[smem] * 2 + [vmem] * 4,
-        out_specs=(vmem,) * 4,
+        out_specs=(vmem, vmem, vmem, smem),
         scratch_shapes=[
             pltpu.VMEM((n_resp, block_rows, wide), low),
             pltpu.VMEM((n_resp, block_rows, wide), low),
@@ -581,25 +671,29 @@
             pltpu.VMEM((hd, period), full),
             pltpu.VMEM((period, wide), low),
             pltpu.VMEM((wide, period), low),
+            pltpu.VMEM((members, positions, wide), low),
+            pltpu.VMEM((members, positions, wide), low),
             pltpu.VMEM((wide, span), low),
             pltpu.VMEM((wide, span), low),
             pltpu.VMEM((members, wide, positions), low),
             pltpu.VMEM((members, wide, positions), low),
             pltpu.VMEM((span, period), full),
             pltpu.VMEM((members, positions, period), full),
-            pltpu.VMEM((count, span, TILE), full),
-            pltpu.VMEM((count, positions, TILE), full),
-            pltpu.VMEM((count, span, TILE), low),
+            pltpu.VMEM((span + positions, count * TILE), low),
+            pltpu.VMEM((count * TILE, wide), low),
+            pltpu.VMEM((count * TILE, wide), low),
+            pltpu.VMEM((16, TILE), full),
             pltpu.VMEM((16, TILE), full),
             pltpu.VMEM((8, TILE), full),
             pltpu.VMEM((members, rows, hd), full),
-            pltpu.VMEM((2, span, wide), full),
-            pltpu.VMEM((members, 2, positions, wide), full),
             pltpu.VMEM((n_tensor, 8 * members, hd), full),
+            pltpu.VMEM((n_prompt, 8, hd), full),
+            pltpu.VMEM((n_prompt * n_resp, hd), full),
             pltpu.VMEM((2, span, wide), low),
             pltpu.VMEM((2, n_prompt, block_rows, wide), low),
             pltpu.VMEM((2, LONG, WIDE, block_rows, wide), low),
             pltpu.VMEM((2, LONG, block_rows, wide), low),
+            pltpu.VMEM((members, 2, positions, wide), full),
             pltpu.VMEM((2, 2, LONG, half, wide), low),
             pltpu.VMEM((2, 2, LONG, block_rows, wide), low),
             pltpu.VMEM((2, 2, half, wide), low),
@@ -607,6 +701,8 @@
             *ways(),
             dma((n_tensor - 1,)),
             dma((n_tensor - 1,)),
+            dma((n_prompt,)),
+            dma((n_prompt,)),
             *ways(),
         ],
         compiler_params=pltpu.CompilerParams(
@@ -615,35 +711,22 @@
     )(prompt_of, prompt_len, q, own, rkv, w)
 
 
-def pack(kv):
-    flat = jnp.moveaxis(kv, -2, -4)
-    return flat.reshape(flat.shape[:-2] + (-1,))
-
-
-def unpack(flat, kv_heads):
-    split = flat.reshape(flat.shape[:-1] + (kv_heads, -1))
-    return jnp.moveaxis(split, -4, -2)
-
-
 def shards(queries, resp_kv, prompt_kv, prompt_of, prompt_len, reward_head):
     _, members, positions, heads, hd = queries.shape
-    kv_heads = prompt_kv.shape[2]
-    q = queries.reshape(members, positions * heads, hd)
-    gq, gr, owned, margin = pair_call(
+    gq, gr, owned, pair_loss = pair_call(
         prompt_of,
         prompt_len,
-        q,
-        pack(prompt_kv[0]),
-        pack(resp_kv[0]),
+        queries.reshape(members, positions * heads, hd),
+        prompt_kv.reshape(prompt_kv.shape[1], -1),
+        resp_kv.reshape(members, positions, -1),
         reward_head,
         lax.axis_size("tensor"),
     )
-    pair_loss = jnp.logaddexp(0.0, margin[0, :1])
     return (
         pair_loss,
         gq.reshape(queries.shape),
-        unpack(gr, kv_heads)[None],
-        unpack(owned, kv_heads)[None],
+        gr.reshape(resp_kv.shape),
+        owned.reshape(prompt_kv.shape),
     )
 
 

time: 132 us -> 126 us (0.955)
  the two profiles are of different devices: /device:TPU:24 before, /device:TPU:8 now
where the time goes in v4:
time: 126 us
  Pallas kernels  116 us (92%)
  local copies, waits for them, and re-layouts  6.78 us (5%)
  between operations  2.42 us (2%)
    pallas_call x1, Pallas kernels, pair_call(): pl.pallas_call(pair_kernel, out_shape=(jax.ShapeDtypeStruct((members, row...  116 us

profile of v4, /device:TPU:8, one launch (start us, length us, event | category | flops | bytes accessed | tf_op | source)
XLA Modules:
  0.0 125.7 jit_solution(1986063063879594427)
XLA Ops:
  0.6 0.0 copy-start
  0.6 1.7 %reshape.28.rkv_ref = bf16[2,64,512]{2,1,0:T(8,128)(2,1)} reshape(bf16[1,2,64,2,2,128]{5,4,3,2,1,0:T(2,128)(2,1)} %param.7) | data formatting | bytes 262144 | tf_op jit(solution)/shard_map/reshape | solution.py:721
  2.3 0.0 copy-done
  2.3 0.7 reshape.27.own_ref
  3.0 116.5 %shard_map.93 = (bf16[2,1536,128]{2,1,0:T(8,128)(2,1)}, bf16[2,64,512]{2,1,0:T(8,128)(2,1)}, bf16[128,512]{1,0:T(8,128)(2,1)}, f32[1]{0:T(128)}) custom-call(s32[128]{0:T(128)} %prompt_of_ref.1, s32[16]{0:T(128)} %prompt_len_ref.1, bf16[2,1536,128]{2,1,0:T(8,128)(2,1)} %bitcast.2, bf16[128,512]{1,0:T(8,128)(2,1)} %reshape.27.own_ref, ...), custom_call_target="tpu_custom_call" | custom-call | tf_op jit(solution)/shard_map/pallas_call | solution.py:653
  119.5 0.0 copy-start.1
  119.5 1.6 %reshape.30 = bf16[1,2,64,2,2,128]{5,4,3,2,1,0:T(2,128)(2,1)} reshape(bf16[2,64,512]{2,1,0:T(8,128)(2,1)} %get-tuple-element.10) | data formatting | bytes 262144 | tf_op jit(solution)/shard_map/reshape | solution.py:728
  121.1 0.0 copy-done.1
  121.1 0.7 reshape.31
  122.5 2.1 %copy.13 = bf16[1,2,64,24,128]{4,3,2,1,0:T(8,128)(2,1)} copy(bf16[1,2,64,24,128]{4,3,2,1,0:T(8,128)(2,1)} %bitcast.3) | data formatting | bytes 1572864
Async XLA Ops:
  0.6 1.7 %copy-start = (bf16[1,128,2,2,128]{4,3,2,1,0:T(2,128)(2,1)S(1)}, bf16[1,128,2,2,128]{4,3,2,1,0:T(2,128)(2,1)}, u32[]{:S(2)}) copy-start(bf16[1,128,2,2,128]{4,3,2,1,0:T(2,128)(2,1)} %param.8) | copy-start | bytes 393220
  119.5 1.6 %copy-start.1 = (bf16[128,512]{1,0:T(8,128)(2,1)S(1)}, bf16[128,512]{1,0:T(8,128)(2,1)}, u32[]{:S(2)}) copy-start(bf16[128,512]{1,0:T(8,128)(2,1)} %get-tuple-element.11) | copy-start | bytes 393220

commit v5 on v4

--- a/solution.py
+++ b/solution.py
@@ -63,11 +63,11 @@
 def pair_kernel(
     prompt_of_ref,
     prompt_len_ref,
-    q_ref,
+    q_hbm_ref,
     own_ref,
     rkv_ref,
     w_ref,
-    gq_ref,
+    gq_hbm_ref,
     gr_ref,
     owned_ref,
     loss_ref,
@@ -75,6 +75,8 @@
     all_v_ref,
     out_ref,
     whole_ref,
+    q_ref,
+    gq_ref,
     wrow_ref,
     wt_ref,
     mask_ref,
@@ -104,7 +106,6 @@
     dense_ref,
     sum_ref,
     grf_ref,
-    x1_ref,
     x2_ref,
     z1_ref,
     z2_ref,
@@ -124,6 +125,7 @@
     xb_recv,
     cb_send,
     cb_recv,
+    io_sem,
 ):
     members, rows, hd = q_ref.shape
     block_rows = own_ref.shape[0]
@@ -152,12 +154,16 @@
             low = (2 * g + part) * hd
             ref[:, low : low + hd] = value[:, g * hd : (g + 1) * hd]
 
+    q_copy = pltpu.make_async_copy(q_hbm_ref, q_ref, io_sem.at[0])
+    q_copy.start()
     me = Place()
     core = me.core
     half = block_rows // 2
     parts = (pl.ds(0, half), pl.ds(half, half))
     up, down = me.at(LONG, 0, core), me.at(-LONG, 0, core)
     right, left = me.at(0, 1, core), me.at(0, -1, core)
+    across = me.at(0, 2, core)
+    sides = (right, left, across)
     far = 2 - 4 * core
     here = me.at(0, 0, core)
     peers = [
@@ -168,6 +174,7 @@
         [up, down, right, left, me.at(0, 0, 1 - core)]
         + [me.at(dz, 0, c) for dz in (1, -1) for c in range(2)]
         + [me.at(-2, 0, 0), me.at(2, 0, 1), me.at(far, 0, core)]
+        + [across]
         + peers
     )
     for device in friends:
@@ -191,17 +198,9 @@
 
     def spread(part, order, dzh):
         block = tables[part].at[slot(dzh, 0)]
-        for side, target in enumerate((right, left)):
+        for side, target in enumerate(sides):
             index = 4 * order + side
             push(block, block, x_send.at[part, index], x_recv.at[part, index], target)
-
-    def relay(part, order, dzh):
-        for side, (dx, target) in enumerate(((-1, right), (1, left))):
-            block = tables[part].at[slot(dzh, dx)]
-            landed(block, x_recv.at[part, 4 * order + side])
-            section = block.at[parts[side]]
-            index = 4 * order + 2 + side
-            push(section, section, x_send.at[part, index], x_recv.at[part, index], target)
 
     def begin(part):
         tables[part][slot(0, 0)] = pick(own_ref[...], part)
@@ -220,7 +219,6 @@
     def middle(part):
         spread(part, 1, -1)
         spread(part, 2, 1)
-        relay(part, 0, 0)
 
     def opposite(part):
         block = tables[part].at[slot(2, 0)]
@@ -228,15 +226,10 @@
             landed(block.at[parts[side]], z_recv.at[part, 2 + side])
         spread(part, 3, 2)
 
-    def relays(part):
-        for order, dzh in ((1, -1), (2, 1), (3, 2)):
-            relay(part, order, dzh)
-
     def complete(part):
-        for order, dzh in ((0, 0), (1, -1), (2, 1), (3, 2)):
-            block = tables[part].at[slot(dzh, 2)]
-            for side in range(2):
-                landed(block.at[parts[side]], x_recv.at[part, 4 * order + 2 + side])
+        for order, dzh in enumerate((0, -1, 1, 2)):
+            for side, dx in enumerate((-1, 1, 2)):
+                landed(tables[part].at[slot(dzh, dx)], x_recv.at[part, 4 * order + side])
 
     def place(device_block):
         return pl.ds(pl.multiple_of(device_block * block_rows, block_rows), block_rows)
@@ -293,13 +286,11 @@
     begin(1)
     middle(0)
     opposite(0)
-    relays(0)
     turn(1)
+    middle(1)
     complete(0)
     deliver(0)
-    middle(1)
     opposite(1)
-    relays(1)
     complete(1)
     deliver(1)
 
@@ -429,6 +420,7 @@
     receive(0)
     for strip in strips:
         kt_ref[:, strip] = whole_ref[0, strip, :].astype(jnp.float32).T.astype(jnp.bfloat16)
+    q_copy.wait()
     run(score_step, 0, count)
     sums(1, halves)
     receive(1)
@@ -445,7 +437,7 @@
         push(ballot, ballot, y_send.at[step], y_recv.at[step], target)
     resp_sums(1)
     dp_ref[...] = product(whole_ref[1], w2t_ref[...])
-    run(back_step, 0, 4)
+    run(back_step, 0, 6)
 
     for step in range(1, n_tensor):
         source = lax.rem(me.tensor + n_tensor - step, n_tensor)
@@ -521,38 +513,21 @@
 
         lax.fori_loop(0, block_rows // chunk, select, 0)
         for order, dzh in enumerate(turns):
-            for side, target in enumerate((right, left)):
+            for side, (dx, target) in enumerate(zip((1, 3, 2), sides)):
                 push(
-                    dense_ref.at[part, dzh, 2, parts[side]],
-                    x1_ref.at[part, side, dzh],
+                    dense_ref.at[part, dzh, dx],
+                    x2_ref.at[part, side, dzh],
                     xb_send.at[part, 4 * order + side],
                     xb_recv.at[part, 4 * order + side],
                     target,
                 )
 
-    def x_turn(part, order):
-        dzh = turns[order]
-        for side, (dx, target) in enumerate(((1, right), (3, left))):
-            arrival = x1_ref.at[part, side, dzh]
-            landed(arrival, xb_recv.at[part, 4 * order + side])
-            block = dense_ref.at[part, dzh, dx]
-            section = block.at[parts[side]]
-            section[...] = add(section, arrival).astype(jnp.bfloat16)
-            index = 4 * order + 2 + side
-            push(
-                block,
-                x2_ref.at[part, side, dzh],
-                xb_send.at[part, index],
-                xb_recv.at[part, index],
-                target,
-            )
-
     def x_end(part, order):
         dzh = turns[order]
-        for side in range(2):
-            landed(x2_ref.at[part, side, dzh], xb_recv.at[part, 4 * order + 2 + side])
+        for side in range(WIDE - 1):
+            landed(x2_ref.at[part, side, dzh], xb_recv.at[part, 4 * order + side])
         total = add(x2_ref.at[part, 0, dzh], x2_ref.at[part, 1, dzh])
-        total += dense_ref[part, dzh, 0].astype(jnp.float32)
+        total += add(x2_ref.at[part, 2, dzh], dense_ref.at[part, dzh, 0])
         sum_ref[part, dzh] = total.astype(jnp.bfloat16)
 
     def z_begin(part):
@@ -587,21 +562,11 @@
         total += sum_ref[part, 0].astype(jnp.float32)
         unpick(owned_ref, part, total.astype(jnp.bfloat16))
 
-    run(back_step, 4, 8)
+    run(back_step, 6, 12)
+    sums(0, halves)
+    give(0)
     factors()
     collect(1)
-    run(back_step, 8, 10)
-    for order in range(LONG):
-        x_turn(1, order)
-    run(back_step, 10, 12)
-    sums(0, halves)
-    give(0)
-    x_end(1, 0)
-    z_begin(1)
-    x_end(1, 1)
-    x_end(1, 2)
-    z_turn(1)
-    x_end(1, 3)
     resp_sums(0)
 
     def write_step(index):
@@ -612,21 +577,28 @@
         )
 
     run(write_step, 0, count)
+    gq_copy = pltpu.make_async_copy(gq_ref, gq_hbm_ref, io_sem.at[1])
+    gq_copy.start()
     gain2 = jnp.concatenate([gain[:1], gain[:1]], axis=1)
     for member in range(members):
         for part in range(2):
             unpick(gr_ref.at[member], part, (grf_ref[member, part] * gain2).astype(jnp.bfloat16))
+    x_end(1, 0)
+    z_begin(1)
     collect(0)
-    z_end(1)
-    for order in range(LONG):
-        x_turn(0, order)
+    x_end(1, 1)
+    x_end(1, 2)
+    z_turn(1)
+    x_end(1, 3)
     x_end(0, 0)
     z_begin(0)
     x_end(0, 1)
     x_end(0, 2)
     z_turn(0)
     x_end(0, 3)
+    z_end(1)
     z_end(0)
+    gq_copy.wait()
     for copy in sent:
         copy.wait_send()
 
@@ -644,6 +616,7 @@
     half = block_rows // 2
     vmem = pl.BlockSpec(memory_space=pltpu.VMEM)
     smem = pl.BlockSpec(memory_space=pltpu.SMEM)
+    hbm = pl.BlockSpec(memory_space=pl.ANY)
     dma = pltpu.SemaphoreType.DMA
     low, full = jnp.bfloat16, jnp.float32
 
@@ -658,13 +631,15 @@
             jax.ShapeDtypeStruct((block_rows, 2 * wide), low),
             jax.ShapeDtypeStruct((1,), full),
         ),
-        in_specs=[smem] * 2 + [vmem] * 4,
-        out_specs=(vmem, vmem, vmem, smem),
+        in_specs=[smem, smem, hbm, vmem, vmem, vmem],
+        out_specs=(hbm, vmem, vmem, smem),
         scratch_shapes=[
             pltpu.VMEM((n_resp, block_rows, wide), low),
             pltpu.VMEM((n_resp, block_rows, wide), low),
             pltpu.VMEM((2, n_prompt - 1, block_rows, wide), low),
             pltpu.VMEM((2, span, wide), low),
+            pltpu.VMEM((members, rows, hd), low),
+            pltpu.VMEM((members, rows, hd), low),
             pltpu.VMEM((period, hd), full),
             pltpu.VMEM((hd, period), full),
             pltpu.VMEM((period, hd), low),
@@ -694,8 +669,7 @@
             pltpu.VMEM((2, LONG, WIDE, block_rows, wide), low),
             pltpu.VMEM((2, LONG, block_rows, wide), low),
             pltpu.VMEM((members, 2, positions, wide), full),
-            pltpu.VMEM((2, 2, LONG, half, wide), low),
-            pltpu.VMEM((2, 2, LONG, block_rows, wide), low),
+            pltpu.VMEM((2, WIDE - 1, LONG, block_rows, wide), low),
             pltpu.VMEM((2, 2, half, wide), low),
             pltpu.VMEM((2, 2, block_rows, wide), low),
             *ways(),
@@ -704,6 +678,7 @@
             dma((n_prompt,)),
             dma((n_prompt,)),
             *ways(),
+            dma((2,)),
         ],
         compiler_params=pltpu.CompilerParams(
             collective_id=0, has_side_effects=True, vmem_limit_bytes=56 * 2**20

time: 126 us -> 112 us (0.89)
  the two profiles are of different devices: /device:TPU:8 before, /device:TPU:1 now
where the time goes in v5:
time: 112 us; the launch traced here: 111 us
  Pallas kernels  102 us (91%)
  local copies, waits for them, and re-layouts  6.78 us (6%)
  between operations  2.42 us (2%)
    pallas_call x1, Pallas kernels, pair_call(): pl.pallas_call(pair_kernel, out_shape=(jax.ShapeDtypeStruct((members, row...  102 us

profile of v5, /device:TPU:1, one launch (start us, length us, event | category | flops | bytes accessed | tf_op | source)
XLA Modules:
  0.0 111.4 jit_solution(6158992052867016122)
XLA Ops:
  0.6 0.0 copy-start
  0.6 1.7 %reshape.28.rkv_ref = bf16[2,64,512]{2,1,0:T(8,128)(2,1)} reshape(bf16[1,2,64,2,2,128]{5,4,3,2,1,0:T(2,128)(2,1)} %param.7) | data formatting | bytes 262144 | tf_op jit(solution)/shard_map/reshape | solution.py:696
  2.3 0.0 copy-done
  2.3 0.7 reshape.27.own_ref
  3.0 102.2 %shard_map.93 = (bf16[2,1536,128]{2,1,0:T(8,128)(2,1)}, bf16[2,64,512]{2,1,0:T(8,128)(2,1)}, bf16[128,512]{1,0:T(8,128)(2,1)}, f32[1]{0:T(128)}) custom-call(s32[128]{0:T(128)} %prompt_of_ref.1, s32[16]{0:T(128)} %prompt_len_ref.1, bf16[2,1536,128]{2,1,0:T(8,128)(2,1)} %bitcast.2, bf16[128,512]{1,0:T(8,128)(2,1)} %reshape.27.own_ref, ...), custom_call_target="tpu_custom_call" | custom-call | tf_op jit(solution)/shard_map/pallas_call | solution.py:626
  105.2 0.0 copy-start.1
  105.2 1.6 %reshape.30 = bf16[1,2,64,2,2,128]{5,4,3,2,1,0:T(2,128)(2,1)} reshape(bf16[2,64,512]{2,1,0:T(8,128)(2,1)} %get-tuple-element.10) | data formatting | bytes 262144 | tf_op jit(solution)/shard_map/reshape | solution.py:703
  106.9 0.0 copy-done.1
  106.9 0.7 reshape.31
  108.2 2.1 %copy.13 = bf16[1,2,64,24,128]{4,3,2,1,0:T(8,128)(2,1)} copy(bf16[1,2,64,24,128]{4,3,2,1,0:T(8,128)(2,1)} %bitcast.3) | data formatting | bytes 1572864
Async XLA Ops:
  0.6 1.7 %copy-start = (bf16[1,128,2,2,128]{4,3,2,1,0:T(2,128)(2,1)S(1)}, bf16[1,128,2,2,128]{4,3,2,1,0:T(2,128)(2,1)}, u32[]{:S(2)}) copy-start(bf16[1,128,2,2,128]{4,3,2,1,0:T(2,128)(2,1)} %param.8) | copy-start | bytes 393220
  105.2 1.6 %copy-start.1 = (bf16[128,512]{1,0:T(8,128)(2,1)S(1)}, bf16[128,512]{1,0:T(8,128)(2,1)}, u32[]{:S(2)}) copy-start(bf16[128,512]{1,0:T(8,128)(2,1)} %get-tuple-element.11) | copy-start | bytes 393220

commit v6 on v5

--- a/solution.py
+++ b/solution.py
@@ -92,6 +92,7 @@
     dp_ref,
     drp_ref,
     low_ref,
+    ds_ref,
     w2i_ref,
     q2i_ref,
     inverse_ref,
@@ -145,10 +146,6 @@
     keys = pl.ds(0, span)
     tail = pl.ds(span, positions)
 
-    def pick(flat, part):
-        lows = [slice((2 * g + part) * hd, (2 * g + part + 1) * hd) for g in range(2)]
-        return jnp.concatenate([flat[:, low] for low in lows], axis=1)
-
     def unpick(ref, part, value):
         for g in range(2):
             low = (2 * g + part) * hd
@@ -203,7 +200,9 @@
             push(block, block, x_send.at[part, index], x_recv.at[part, index], target)
 
     def begin(part):
-        tables[part][slot(0, 0)] = pick(own_ref[...], part)
+        mine = slot(0, 0)
+        for g in range(2):
+            tables[part][mine, :, g * hd : (g + 1) * hd] = own_ref[:, g, part, :]
         block = tables[part].at[slot(0, 0)]
         push(block, block, z_send.at[part, 0], z_recv.at[part, 0], up)
         push(block, block, z_send.at[part, 1], z_recv.at[part, 1], down)
@@ -275,8 +274,10 @@
         w2_ref[part, :] = w2.astype(jnp.bfloat16)
         w2t_ref[:, part] = w2.T.astype(jnp.bfloat16)
     for member in range(members):
-        rk_ref[member] = pick(rkv_ref[member], 0)
-        rv_ref[member] = pick(rkv_ref[member], 1)
+        for g in range(2):
+            low = slice(g * hd, (g + 1) * hd)
+            rk_ref[member, :, low] = rkv_ref[member, :, g, 0, :]
+            rv_ref[member, :, low] = rkv_ref[member, :, g, 1, :]
         rkt_ref[member] = rk_ref[member].astype(jnp.float32).T.astype(jnp.bfloat16)
         rvt_ref[member] = rv_ref[member].astype(jnp.float32).T.astype(jnp.bfloat16)
         drp_ref[member] = product(rv_ref[member], w2t_ref[...])
@@ -377,34 +378,40 @@
     def back_step(index):
         member, start, lane, column, sign = where_is(index)
         delta = delta_ref[pl.ds(index, 1), :]
-        for strip in strips:
-            low_ref[strip, column] = low_ref[strip, column] * (dp_ref[strip, lane] - delta).astype(
-                jnp.bfloat16
-            )
+        ds = jnp.concatenate(
+            [
+                low_ref[strip, column] * (dp_ref[strip, lane] - delta).astype(jnp.bfloat16)
+                for strip in strips
+            ],
+            axis=0,
+        )
         dsr = low_ref[tail, column] * (drp_ref[member, :, lane] - delta).astype(jnp.bfloat16)
-        low_ref[tail, column] = dsr
-        both = product(kt_ref[...], low_ref[keys, column]) + product(rkt_ref[member], dsr)
+        ds_ref[keys, column] = ds
+        ds_ref[tail, column] = dsr
+        both = product(kt_ref[...], ds) + product(rkt_ref[member], dsr)
         gq = jnp.where(mask_t_ref[:, lane] > 0.5, both[:hd], both[hd:])
         gq = gq * (inverse_ref[pl.ds(index, 1), :] * (sign * scale))
         gqf_ref[member, pl.ds(start, TILE), :] = gq.T
 
-    def sums(part, left):
-        right_ref = (q2i_ref, w2i_ref)[part]
-        factor = 1.0 if part else scale
-        for strip in left:
-            value = product(low_ref[strip, :], right_ref[...]) * factor
-            piece_ref[part, strip, :] = value.astype(jnp.bfloat16)
-
     def resp_sums(part):
-        right_ref = (q2i_ref, w2i_ref)[part]
+        left_ref, right_ref = ((ds_ref, q2i_ref), (low_ref, w2i_ref))[part]
         factor = 1.0 if part else scale
         for member in range(members):
             column = slice(member * rows, (member + 1) * rows)
-            grf_ref[member, part] = product(low_ref[tail, column], right_ref[column, :]) * factor
-
-    def give(part):
+            grf_ref[member, part] = product(left_ref[tail, column], right_ref[column, :]) * factor
+
+    def sums(part):
+        left_ref, right_ref = ((ds_ref, q2i_ref), (low_ref, w2i_ref))[part]
+        factor = 1.0 if part else scale
+        for kind, dz in ((3, 2), (1, 1), (2, -1), (0, 0)):
+            row = pl.ds(pl.multiple_of(me.block(dz, 0) * block_rows, block_rows), 2 * block_rows)
+            value = product(left_ref[row, :], right_ref[...]) * factor
+            piece_ref[part, row, :] = value.astype(jnp.bfloat16)
+            yield kind, dz
+
+    def give(part, ready):
         index = 0
-        for kind, dz in ((3, 2), (1, 1), (2, -1), (0, 0)):
+        for kind, dz in ready:
             for c in range(2) if kind else (1 - core,):
                 push(
                     piece_ref.at[part, place(me.block(dz, c))],
@@ -416,15 +423,14 @@
                 index += 1
         got_ref[part, core] = piece_ref[part, place(me.block(0, core)), :]
 
-    halves = [slice(0, span // 2), slice(span // 2, span)]
     receive(0)
     for strip in strips:
         kt_ref[:, strip] = whole_ref[0, strip, :].astype(jnp.float32).T.astype(jnp.bfloat16)
     q_copy.wait()
     run(score_step, 0, count)
-    sums(1, halves)
+    value_pieces = list(sums(1))
     receive(1)
-    give(1)
+    give(1, value_pieces)
     for strip in strips:
         vt_ref[:, strip] = whole_ref[1, strip, :].astype(jnp.float32).T.astype(jnp.bfloat16)
     run(out_step, 0, count)
@@ -435,7 +441,6 @@
         ballot[8 * member : 8 * (member + 1), :] = jnp.broadcast_to(total, (8, hd))
     for step, target in enumerate(peers):
         push(ballot, ballot, y_send.at[step], y_recv.at[step], target)
-    resp_sums(1)
     dp_ref[...] = product(whole_ref[1], w2t_ref[...])
     run(back_step, 0, 6)
 
@@ -493,26 +498,26 @@
             for c in range(2) if kind else (1 - core,):
                 landed(got_ref.at[part, 2 * kind + c], cb_recv.at[part, 2 * kind + c])
 
-        def select(index, carry):
-            row = pl.ds(pl.multiple_of(index * chunk, chunk), chunk)
-            for start in range(0, wide, lanes):
-                column = slice(start, start + lanes)
-                terms = [
-                    got_ref[part, source, row, column].astype(jnp.float32)
-                    for source in range(sources)
-                ]
-                for a in range(LONG):
+        for order, dzh in enumerate(turns):
+
+            def select(index, carry):
+                row = pl.ds(pl.multiple_of(index * chunk, chunk), chunk)
+                for start in range(0, wide, lanes):
+                    column = slice(start, start + lanes)
+                    terms = [
+                        got_ref[part, source, row, column].astype(jnp.float32)
+                        for source in range(sources)
+                    ]
                     for b in range(WIDE):
-                        base = (a * WIDE + b) * sources
+                        base = (dzh * WIDE + b) * sources
                         total = terms[0] * factor_ref[base : base + 1, :]
                         for source in range(1, sources):
                             at = base + source
                             total += terms[source] * factor_ref[at : at + 1, :]
-                        dense_ref[part, a, b, row, column] = total.astype(jnp.bfloat16)
-            return carry
-
-        lax.fori_loop(0, block_rows // chunk, select, 0)
-        for order, dzh in enumerate(turns):
+                        dense_ref[part, dzh, b, row, column] = total.astype(jnp.bfloat16)
+                return carry
+
+            lax.fori_loop(0, block_rows // chunk, select, 0)
             for side, (dx, target) in enumerate(zip((1, 3, 2), sides)):
                 push(
                     dense_ref.at[part, dzh, dx],
@@ -563,11 +568,11 @@
         unpick(owned_ref, part, total.astype(jnp.bfloat16))
 
     run(back_step, 6, 12)
-    sums(0, halves)
-    give(0)
+    give(0, sums(0))
     factors()
     collect(1)
     resp_sums(0)
+    resp_sums(1)
 
     def write_step(index):
         member, start, lane, column, sign = where_is(index)
@@ -581,8 +586,10 @@
     gq_copy.start()
     gain2 = jnp.concatenate([gain[:1], gain[:1]], axis=1)
     for member in range(members):
-        for part in range(2):
-            unpick(gr_ref.at[member], part, (grf_ref[member, part] * gain2).astype(jnp.bfloat16))
+        pair = [(grf_ref[member, part] * gain2).astype(jnp.bfloat16) for part in range(2)]
+        for g in range(2):
+            low = slice(g * hd, (g + 1) * hd)
+            gr_ref[member, :, g, :, :] = jnp.stack([each[:, low] for each in pair], axis=1)
     x_end(1, 0)
     z_begin(1)
     collect(0)
@@ -606,7 +613,7 @@
 def pair_call(prompt_of, prompt_len, q, own, rkv, w, n_tensor):
     members, rows, hd = q.shape
     block_rows = own.shape[0]
-    wide = own.shape[1] // 2
+    wide = 2 * hd
     positions = rkv.shape[1]
     heads = w.shape[0]
     n_prompt, n_resp = 2 * LONG, LONG * WIDE
@@ -627,7 +634,7 @@
         pair_kernel,
         out_shape=(
             jax.ShapeDtypeStruct((members, rows, hd), low),
-            jax.ShapeDtypeStruct((members, positions, 2 * wide), low),
+            jax.ShapeDtypeStruct((members, positions, 2, 2, hd), low),
             jax.ShapeDtypeStruct((block_rows, 2 * wide), low),
             jax.ShapeDtypeStruct((1,), full),
         ),
@@ -654,6 +661,7 @@
             pltpu.VMEM((members, wide, positions), low),
             pltpu.VMEM((span, period), full),
             pltpu.VMEM((members, positions, period), full),
+            pltpu.VMEM((span + positions, count * TILE), low),
             pltpu.VMEM((span + positions, count * TILE), low),
             pltpu.VMEM((count * TILE, wide), low),
             pltpu.VMEM((count * TILE, wide), low),
@@ -692,8 +700,8 @@
         prompt_of,
         prompt_len,
         queries.reshape(members, positions * heads, hd),
-        prompt_kv.reshape(prompt_kv.shape[1], -1),
-        resp_kv.reshape(members, positions, -1),
+        prompt_kv[0],
+        resp_kv[0],
         reward_head,
         lax.axis_size("tensor"),
     )

time: 112 us -> 110 us (0.982)
  local copies, waits for them, and re-layouts: 6.78 us -> 4.38 us
    reshape x3 -> x0, local copies, waits for them, and re-layouts: 3.99 us -> none  [the longest x1 1.65 us: shards(): resp_kv.reshape(members, positions, -1)]
    unnamed x5 -> x4, local copies, waits for them, and re-layouts: 2.1 us -> 2.79 us
where the time goes in v6:
time: 110 us
  Pallas kernels  103 us (94%)
  local copies, waits for them, and re-layouts  4.38 us (4%)
  between operations  2.42 us (2%)
    pallas_call x1, Pallas kernels, pair_call(): pl.pallas_call(pair_kernel, out_shape=(jax.ShapeDtypeStruct((members, row...  103 us
    unnamed x4, local copies, waits for them, and re-layouts  2.79 us

profile of v6, /device:TPU:1, one launch (start us, length us, event | category | flops | bytes accessed | tf_op | source)
XLA Modules:
  0.0 109.5 jit_solution(14950284260471155137)
XLA Ops:
  0.6 102.7 %shard_map.93 = (bf16[2,1536,128]{2,1,0:T(8,128)(2,1)}, bf16[2,64,2,2,128]{4,3,2,1,0:T(2,128)(2,1)}, bf16[128,512]{1,0:T(8,128)(2,1)}, f32[1]{0:T(128)}) custom-call(s32[128]{0:T(128)} %prompt_of_ref.1, s32[16]{0:T(128)} %prompt_len_ref.1, bf16[2,1536,128]{2,1,0:T(8,128)(2,1)} %bitcast.5, bf16[128,2,2,128]{3,2,1,0:T(2,128)(2,1)} %bitcast.7, ...), custom_call_target="tpu_custom_call" | custom-call | tf_op jit(solution)/shard_map/pallas_call | solution.py:633
  103.4 1.6 %reshape.23 = bf16[1,128,2,2,128]{4,3,2,1,0:T(2,128)(2,1)} reshape(bf16[128,512]{1,0:T(8,128)(2,1)} %get-tuple-element.11) | data formatting | bytes 262144 | tf_op jit(solution)/shard_map/reshape | solution.py:712
  105.6 0.0 copy-start
  105.6 2.1 %copy.14 = bf16[1,2,64,24,128]{4,3,2,1,0:T(8,128)(2,1)} copy(bf16[1,2,64,24,128]{4,3,2,1,0:T(8,128)(2,1)} %bitcast.6) | data formatting | bytes 1572864
  107.7 0.0 copy-done
  107.7 0.7 copy.15
Async XLA Ops:
  105.6 2.1 %copy-start = (bf16[2,64,2,2,128]{4,3,2,1,0:T(2,128)(2,1)S(1)}, bf16[2,64,2,2,128]{4,3,2,1,0:T(2,128)(2,1)}, u32[]{:S(2)}) copy-start(bf16[2,64,2,2,128]{4,3,2,1,0:T(2,128)(2,1)} %get-tuple-element.10) | copy-start | bytes 393220

commit v7 on v6

--- a/solution.py
+++ b/solution.py
@@ -146,11 +146,6 @@
     keys = pl.ds(0, span)
     tail = pl.ds(span, positions)
 
-    def unpick(ref, part, value):
-        for g in range(2):
-            low = (2 * g + part) * hd
-            ref[:, low : low + hd] = value[:, g * hd : (g + 1) * hd]
-
     q_copy = pltpu.make_async_copy(q_hbm_ref, q_ref, io_sem.at[0])
     q_copy.start()
     me = Place()
@@ -565,7 +560,7 @@
             landed(z2_ref.at[part, side], zb_recv.at[part, 2 + side])
         total = add(z2_ref.at[part, 0], z2_ref.at[part, 1])
         total += sum_ref[part, 0].astype(jnp.float32)
-        unpick(owned_ref, part, total.astype(jnp.bfloat16))
+        sum_ref[part, 0] = total.astype(jnp.bfloat16)
 
     run(back_step, 6, 12)
     give(0, sums(0))
@@ -605,6 +600,9 @@
     x_end(0, 3)
     z_end(1)
     z_end(0)
+    for g in range(2):
+        low = slice(g * hd, (g + 1) * hd)
+        owned_ref[:, g, :, :] = jnp.stack([sum_ref[part, 0, :, low] for part in range(2)], axis=1)
     gq_copy.wait()
     for copy in sent:
         copy.wait_send()
@@ -635,7 +633,7 @@
         out_shape=(
             jax.ShapeDtypeStruct((members, rows, hd), low),
             jax.ShapeDtypeStruct((members, positions, 2, 2, hd), low),
-            jax.ShapeDtypeStruct((block_rows, 2 * wide), low),
+            jax.ShapeDtypeStruct((block_rows, 2, 2, hd), low),
             jax.ShapeDtypeStruct((1,), full),
         ),
         in_specs=[smem, smem, hbm, vmem, vmem, vmem],

time: 110 us -> 110 us (level)
    reshape x1 -> x0, local copies, waits for them, and re-layouts: 1.59 us -> none  [shards(): owned.reshape(prompt_kv.shape)]
    unnamed x4 -> x7, local copies, waits for them, and re-layouts: 2.79 us -> 3.74 us
where the time goes in v7:
time: 110 us
  Pallas kernels  103 us (94%)
  local copies, waits for them, and re-layouts  3.74 us (3%)
  between operations  2.41 us (2%)
    pallas_call x1, Pallas kernels, pair_call(): pl.pallas_call(pair_kernel, out_shape=(jax.ShapeDtypeStruct((members, row...  103 us
    unnamed x7, local copies, waits for them, and re-layouts  3.74 us

profile of v7, /device:TPU:1, one launch (start us, length us, event | category | flops | bytes accessed | tf_op | source)
XLA Modules:
  0.0 109.5 jit_solution(13835007188345337744)
XLA Ops:
  0.6 103.4 %shard_map.93 = (bf16[2,1536,128]{2,1,0:T(8,128)(2,1)}, bf16[2,64,2,2,128]{4,3,2,1,0:T(2,128)(2,1)}, bf16[128,2,2,128]{3,2,1,0:T(2,128)(2,1)}, f32[1]{0:T(128)}) custom-call(s32[128]{0:T(128)} %prompt_of_ref.1, s32[16]{0:T(128)} %prompt_len_ref.1, bf16[2,1536,128]{2,1,0:T(8,128)(2,1)} %bitcast.6, bf16[128,2,2,128]{3,2,1,0:T(2,128)(2,1)} %bitcast.8, ...), custom_call_target="tpu_custom_call" | custom-call | tf_op jit(solution)/shard_map/pallas_call | solution.py:631
  104.7 0.0 copy-start.1
  104.7 2.1 %copy.15 = bf16[1,2,64,24,128]{4,3,2,1,0:T(8,128)(2,1)} copy(bf16[1,2,64,24,128]{4,3,2,1,0:T(8,128)(2,1)} %bitcast.7) | data formatting | bytes 1572864
  106.8 0.0 copy-done.1
  106.8 0.0 copy-start
  106.8 0.7 copy.16
  107.5 0.3 copy-done
  107.8 0.7 copy.17
Async XLA Ops:
  104.7 2.1 %copy-start.1 = (bf16[2,64,2,2,128]{4,3,2,1,0:T(2,128)(2,1)S(1)}, bf16[2,64,2,2,128]{4,3,2,1,0:T(2,128)(2,1)}, u32[]{:S(2)}) copy-start(bf16[2,64,2,2,128]{4,3,2,1,0:T(2,128)(2,1)} %get-tuple-element.10) | copy-start | bytes 393220
  106.8 1.0 copy-start
